TPU v7x, 32 devices: a whole 2x2x4 slice. The times are simulated.
32 devices in a mesh: grp: 2 (over y), tile: 16 (over z, x, core).
Axes of the slice: x: 2, y: 2, z: 4, core: 2. Of those that a mesh axis runs over, the one named last changes fastest.
Arguments:
- flux_east: bfloat16 [256, 768, 128], P(None, ('grp', 'tile')), parts along dimension 1, may hold values from -6 to 6
- flux_north: bfloat16 [256, 768, 128], P(None, ('grp', 'tile')), parts along dimension 1, may hold values from -6 to 6
- band_freqs: int32 [96], replicated, may hold values from 1 to 127, as said below
- start_basis: float32 [256, 64], replicated, may hold values from -6 to 6
Outputs:
- rebuilt: bfloat16 [256, 768, 128], P(None, ('grp', 'tile')), parts along dimension 1
There are 2 independent parts, one for each index of `grp`. A program takes and returns all parts, laid end to end along the dimension named above; an argument that names none is the same for every part. Nothing has to cross between parts.
Inputs may be any that keep to these rules, and one draw needn't show every extreme that they name: `band_freqs`: the values are distinct and include 1 and 127.
All inputs are finite; a program needn't handle non-finite values.
Results may differ from a plain program's by a relative error of at most 0.0038.
The roundings to bfloat16 on the way count: a program that leaves them out, or rounds other values in their place, can miss the bound.
Values may be sent and summed in bfloat16 or wider, within the bound.
No kernel may reach another device: no remote copies, remote signals or barrier semaphores. Data moves between devices by JAX's collectives and lax.ppermute only.
A program may use at most 64 MiB of HBM per device.

v0:
```python
import math

import jax
import jax.numpy as jnp
from jax import lax
from jax.sharding import PartitionSpec as P

ITERS = 4


def extended(shard, sides, width):
    for axis, dim in sides:
        peers, length = (lax.axis_size(axis), shard.shape[dim])
        up = [(i, (i + 1) % peers) for i in range(peers - 1)]
        down = [(j, i) for i, j in up]
        last = lax.slice_in_dim(shard, length - width, length, axis=dim)
        leading = lax.slice_in_dim(shard, 0, width, axis=dim)
        before = lax.ppermute(last, axis, up)
        after = lax.ppermute(leading, axis, down)
        shard = jnp.concatenate([before, shard, after], axis=dim)
    return shard


def wave_table(band_freqs, hour_count):
    times = jnp.arange(hour_count, dtype=jnp.int32)
    phase = times[:, None] * band_freqs[None, :] % hour_count
    angles = phase.astype(jnp.float32) * (2.0 * math.pi / hour_count)
    return jnp.concatenate([jnp.cos(angles), jnp.sin(angles)], axis=1).astype(jnp.bfloat16)


def expand(wide, core):
    return jnp.dot(
        jnp.dot(wide, core, precision=lax.Precision.HIGHEST),
        wide.T,
        precision=lax.Precision.HIGHEST,
    )


def orthonormal(panel):
    crossed = jnp.dot(panel.T, panel, precision=lax.Precision.HIGHEST)
    factor = jnp.linalg.cholesky(crossed)
    return jax.scipy.linalg.solve_triangular(factor, panel.T, lower=True).T


def refine(gram, basis):
    for sweep in range(ITERS):
        basis = orthonormal(jnp.dot(gram, basis, precision=lax.Precision.HIGHEST))
    return basis


def body(flux_east, flux_north, band_freqs, start_basis):
    hour_count, row_count, col_count = flux_east.shape
    tile_count = lax.axis_size("tile")
    cell_total = row_count * col_count * tile_count
    factor_scale = (2.0 / hour_count) ** 2 / cell_total
    padded = extended(flux_east, (("tile", 1),), 1)
    northward = jnp.pad(flux_north.astype(jnp.float32), ((0, 0), (0, 0), (1, 1)))
    across = 0.5 * (northward[:, :, 2:] - northward[:, :, :-2])
    eastward = padded.astype(jnp.float32)
    along = 0.5 * (eastward[:, 2:, :] - eastward[:, :-2, :])
    convergence = (along + across).astype(jnp.bfloat16).reshape(hour_count, row_count * col_count)
    table = wave_table(band_freqs, hour_count)
    bands = jnp.dot(table.T, convergence, preferred_element_type=jnp.float32).astype(jnp.bfloat16)
    filtered = (
        jnp.dot(table, bands, preferred_element_type=jnp.float32) * (2.0 / hour_count)
    ).astype(jnp.bfloat16)
    local_core = jnp.dot(bands, bands.T, preferred_element_type=jnp.float32)
    wide = table.astype(jnp.float32)
    local_gram = expand(wide, local_core)
    gram = lax.psum(local_gram, "tile") * factor_scale
    basis = refine(gram, start_basis)
    basis_half = basis.astype(jnp.bfloat16)
    coefficients = jnp.dot(basis_half.T, filtered, preferred_element_type=jnp.float32).astype(
        jnp.bfloat16
    )
    rebuilt = jnp.dot(basis_half, coefficients, preferred_element_type=jnp.float32).astype(
        jnp.bfloat16
    )
    return rebuilt.reshape(hour_count, row_count, col_count)


def solution(mesh):
    placed = (P(None, ("grp", "tile"), None), P(None, ("grp", "tile"), None), P(), P())
    return jax.shard_map(
        body, mesh=mesh, in_specs=placed, out_specs=P(None, ("grp", "tile"), None), check_vma=False
    )
```

profile of v0, /device:TPU:0, one launch (start us, length us, event | category | flops | bytes accessed | tf_op | source)
XLA Modules:
  0.0 177.6 jit_solution(4037550972994099397)
XLA Ops:
  6.5 1.4 fusion.57
  8.0 1.3 collective-permute-start.1
  9.3 3.2 %collective-permute-start = (bf16[256,1,128]{2,1,0:T(2,128)(2,1)S(1)}, bf16[256,1,128]{2,1,0:T(2,128)(2,1)S(1)}, u32[]{:S(2)}, u32[]{:S(2)}) collective-permute-start(bf16[256,1,128]{2,1,0:T(2,128)(2,1)S(1)} %get-tuple-element.6), channel_id=1, source_target_pairs={{0,1},{1,2},{2,3},{3,4},{4,5},{5,6},{6,7},{7,8},{8,9},{9,10},{10,1... | collective-permute-start | bytes 196616 | tf_op jit(solution)/shard_map/ppermute | solution.py:18
  12.5 2.3 %pad_convert_fusion = f32[256,24,130]{2,1,0:T(8,128)S(1)} fusion(bf16[256,24,128]{2,1,0:T(8,128)(2,1)} %param.8), kind=kLoop, calls=%fused_computation.10 | loop fusion | flops 798720 | bytes 4767744 | tf_op jit(solution)/shard_map/jit(_pad)/pad | solution.py:57
  15.4 1.1 maximum_convert_fusion
  16.5 1.1 fusion.3
  18.9 1.1 fusion.55
  20.1 93.4 %all-reduce.3.cloned.1.call-done = f32[256,256]{1,0:T(8,128)} async-done(((f32[256,256]{1,0:T(8,128)}), f32[256,256]{1,0:T(8,128)}) %all-reduce.3.cloned.1.call-update) | async-done | bytes 262160 | tf_op jit(solution)/shard_map/psum | solution.py:70
  113.5 1.4 fusion.13
  115.2 5.8 %cholesky.74 = f32[64,64]{1,0:T(8,128)S(1)} custom-call(f32[64,64]{1,0:T(8,128)S(1)} %fusion.43), custom_call_target="Cholesky" | custom-call | tf_op jit(solution)/shard_map/jit(cholesky)/cholesky | solution.py:41
  121.8 0.7 fusion.32
  122.4 4.9 %custom-call.8 = f32[1,64,64]{1,2,0:T(8,128)S(1)} custom-call(f32[1,64,64]{2,1,0:T(8,128)S(1)} %fusion.32), custom_call_target="InvertDiagBlocksLowerTriangular" | custom-call | tf_op jit(solution)/shard_map/jit(_solve_triangular)/triangular_solve | solution.py:42
  127.6 1.3 fusion.11
  129.2 5.8 %cholesky.85 = f32[64,64]{1,0:T(8,128)S(1)} custom-call(f32[64,64]{1,0:T(8,128)S(1)} %fusion.41), custom_call_target="Cholesky" | custom-call | tf_op jit(solution)/shard_map/jit(cholesky)/cholesky | solution.py:41
  135.8 0.7 fusion.33
  136.4 4.9 %custom-call.9 = f32[1,64,64]{1,2,0:T(8,128)S(1)} custom-call(f32[1,64,64]{2,1,0:T(8,128)S(1)} %fusion.33), custom_call_target="InvertDiagBlocksLowerTriangular" | custom-call | tf_op jit(solution)/shard_map/jit(_solve_triangular)/triangular_solve | solution.py:42
  142.3 5.8 %cholesky.96 = f32[64,64]{1,0:T(8,128)S(1)} custom-call(f32[64,64]{1,0:T(8,128)S(1)} %fusion.39), custom_call_target="Cholesky" | custom-call | tf_op jit(solution)/shard_map/jit(cholesky)/cholesky | solution.py:41
  148.8 0.7 fusion.34
  149.5 4.9 %custom-call.10 = f32[1,64,64]{1,2,0:T(8,128)S(1)} custom-call(f32[1,64,64]{2,1,0:T(8,128)S(1)} %fusion.34), custom_call_target="InvertDiagBlocksLowerTriangular" | custom-call | tf_op jit(solution)/shard_map/jit(_solve_triangular)/triangular_solve | solution.py:42
  155.5 5.8 %cholesky.107 = f32[64,64]{1,0:T(8,128)S(1)} custom-call(f32[64,64]{1,0:T(8,128)S(1)} %fusion.37), custom_call_target="Cholesky" | custom-call | tf_op jit(solution)/shard_map/jit(cholesky)/cholesky | solution.py:41
  162.0 0.7 fusion.35
  162.7 4.9 %custom-call.11 = f32[1,64,64]{1,2,0:T(8,128)S(1)} custom-call(f32[1,64,64]{2,1,0:T(8,128)S(1)} %fusion.35), custom_call_target="InvertDiagBlocksLowerTriangular" | custom-call | tf_op jit(solution)/shard_map/jit(_solve_triangular)/triangular_solve | solution.py:42
  167.9 0.8 convolution_convert_fusion.2
  169.3 1.5 copy.10
  (43 shorter events, 8.4 us)
Async XLA Ops:
  6.5 107.0 %copy-start = (f32[256,64]{0,1:T(8,128)S(1)}, f32[256,64]{0,1:T(8,128)}, u32[]{:S(2)}) copy-start(f32[256,64]{0,1:T(8,128)} %param.10) | copy-start | bytes 196612
  6.5 107.0 %all-reduce.3.cloned.1.call-start = ((), (), s32[]{:S(2)}) async-start(), calls=%async_computation | async-start | bytes 524288 | tf_op jit(solution)/shard_map/psum | solution.py:70
  8.0 7.4 %collective-permute-start.1 = (bf16[256,1,128]{2,1,0:T(2,128)(2,1)S(1)}, bf16[256,1,128]{2,1,0:T(2,128)(2,1)S(1)}, u32[]{:S(2)}, u32[]{:S(2)}) collective-permute-start(bf16[256,1,128]{2,1,0:T(2,128)(2,1)S(1)} %get-tuple-element.8), channel_id=1, source_target_pairs={{1,0},{2,1},{3,2},{4,3},{5,4},{6,5},{7,6},{8,7},{9,8},{10,9},{11,1... | collective-permute-start | bytes 196616 | tf_op jit(solution)/shard_map/ppermute | solution.py:19
  9.3 5.5 %copy-start.3 = (s32[96]{0:T(128)S(1)}, s32[96]{0:T(128)}, u32[]{:S(2)}) copy-start(s32[96]{0:T(128)} %param.9) | copy-start | bytes 1156
  9.3 6.1 %copy-start.2 = (bf16[256,24,128]{2,1,0:T(8,128)(2,1)S(1)}, bf16[256,24,128]{2,1,0:T(8,128)(2,1)}, u32[]{:S(2)}) copy-start(bf16[256,24,128]{2,1,0:T(8,128)(2,1)} %param.7) | copy-start | bytes 4718596
  9.3 6.1 %collective-permute-start = (bf16[256,1,128]{2,1,0:T(2,128)(2,1)S(1)}, bf16[256,1,128]{2,1,0:T(2,128)(2,1)S(1)}, u32[]{:S(2)}, u32[]{:S(2)}) collective-permute-start(bf16[256,1,128]{2,1,0:T(2,128)(2,1)S(1)} %get-tuple-element.6), channel_id=1, source_target_pairs={{0,1},{1,2},{2,3},{3,4},{4,5},{5,6},{6,7},{7,8},{8,9},{9,10},{10,1... | collective-permute-start | bytes 196616 | tf_op jit(solution)/shard_map/ppermute | solution.py:18
  113.5 28.1 %copy-start.1 = (f32[256,256]{1,0:T(8,128)S(1)}, f32[256,256]{1,0:T(8,128)}, u32[]{:S(2)}) copy-start(f32[256,256]{1,0:T(8,128)} %all-reduce.3.cloned.1.call-done) | copy-start | bytes 786436
Sparse Core Ops, SparseCore 0:
  20.2 93.2 all-reduce.2
where the time goes:
time: 178 us
  waiting for transfers between devices  93.5 us (53%)
  other arithmetic  53.3 us (30%)
  between operations  13.7 us (8%)
  matrix products  9.48 us (5%)
  starting transfers between devices  4.46 us (3%)
  local copies, waits for them, and re-layouts  3.21 us (2%)
    psum x1, waiting for transfers between devices, body(): gram = lax.psum(local_gram, 'tile') * factor_scale  93.4 us
    another operation x12, other arithmetic, orthonormal(): factor = jnp.linalg.cholesky(crossed)  26.1 us
    another operation x8, other arithmetic, orthonormal(): return jax.scipy.linalg.solve_triangular(factor, panel.T, lower=True).T  22.2 us
    dot_general x4, matrix products, refine(): basis = orthonormal(jnp.dot(gram, basis, precision=lax.Precision.HIGHEST))  3.63 us
  transfers between devices with their start and end apart: 3, of which 1 were waited for; matrix products, arithmetic and copies ran while one was open for 2% of the time, Pallas kernels for 0%

commit v1 on v0

v1 whole, which is shorter than its diff:
```python
import functools
import math

import jax
import jax.numpy as jnp
from jax import lax
from jax.experimental import pallas as pl
from jax.experimental.pallas import tpu as pltpu
from jax.sharding import PartitionSpec as P

ITERS = 4
WIDE = 16
EXACT = lax.Precision.HIGHEST


def partners(count, mask):
    return [(i, i ^ mask) for i in range(count)]


def halo_rows(shard, axis):
    count = lax.axis_size(axis)
    even = lax.axis_index(axis) % 2 == 0
    head, tail = shard[:, :1], shard[:, -1:]
    inner = [(i, i + 1) for i in range(0, count - 1, 2)]
    outer = [(i, i + 1) for i in range(1, count - 1, 2)]
    from_outer = lax.ppermute(
        jnp.where(even, head, tail), axis, outer + [(j, i) for i, j in outer]
    )
    from_inner = lax.ppermute(
        jnp.where(even, tail, head), axis, inner + [(j, i) for i, j in inner]
    )
    before = jnp.where(even, from_outer, from_inner)
    after = jnp.where(even, from_inner, from_outer)
    return before, after


def wave_table(band_freqs, hour_count):
    times = jnp.arange(hour_count, dtype=jnp.int32)
    phase = times[:, None] * band_freqs[None, :] % hour_count
    angles = phase.astype(jnp.float32) * (2.0 * math.pi / hour_count)
    return jnp.concatenate([jnp.cos(angles), jnp.sin(angles)], axis=1).astype(jnp.bfloat16)


def packed(core):
    size = core.shape[0] // 3
    right = jnp.concatenate([core[size:, size : 2 * size], core[2 * size :, 2 * size :]], axis=0)
    return jnp.concatenate([core[:, :size], right], axis=1)


def summed_halves(block, axis):
    count = lax.axis_size(axis)
    half = block.shape[0] // 2
    side = lax.axis_index(axis) % 2
    kept = lax.dynamic_slice_in_dim(block, side * half, half)
    given = lax.dynamic_slice_in_dim(block, (1 - side) * half, half)
    kept = kept + lax.ppermute(given, axis, partners(count, 1))
    mask = 2
    while mask < count:
        kept = kept + lax.ppermute(kept, axis, partners(count, mask))
        mask *= 2
    return kept, lax.ppermute(kept, axis, partners(count, 1))


def exact_dot(a, b):
    return lax.dot_general(
        a, b, (((1,), (0,)), ((), ())), precision=EXACT, preferred_element_type=jnp.float32
    )


def exact_dot_t(a, b):
    return lax.dot_general(
        a, b, (((1,), (1,)), ((), ())), precision=EXACT, preferred_element_type=jnp.float32
    )


def lane(v, j):
    return jnp.broadcast_to(v[:, j : j + 1], v.shape)


def row(v, k):
    return jnp.broadcast_to(v[k : k + 1, :], v.shape)


def reciprocal(x):
    guess = pl.reciprocal(x, approx=True)
    return guess * (2.0 - x * guess)


def inverse_factor(crossed):
    size = crossed.shape[0]
    ids = [lax.broadcasted_iota(jnp.int32, (size, size), d) for d in range(2)]
    eye = (ids[0] == ids[1]).astype(jnp.float32)
    joined = jnp.concatenate([crossed, eye], axis=1)
    strips = [joined[s : s + 8] for s in range(0, size, 8)]
    place = lax.broadcasted_iota(jnp.int32, strips[0].shape, 0)
    rows = []
    for start in range(0, size, WIDE):
        first = start // 8
        cols = [[lane(s, start + k) for s in strips[first:]] for k in range(WIDE)]
        for k in range(0, WIDE, 2):
            q, s = k // 8, k % 8
            a, b, c = row(cols[k][q], s), row(cols[k][q], s + 1), row(cols[k + 1][q], s + 1)
            det = a * c - b * b
            inv = reciprocal(det)
            ai, bi, ci = a * inv, b * inv, c * inv
            below = place > s + 1
            u = [jnp.where(below, cols[k][q], 0.0)] + cols[k][q + 1 :]
            v = [jnp.where(below, cols[k + 1][q], 0.0)] + cols[k + 1][q + 1 :]

            def eliminate(target, offset):
                top, low = row(target[offset], s), row(target[offset], s + 1)
                x, y = ci * top - bi * low, ai * low - bi * top
                for i in range(len(u)):
                    target[offset + i] = target[offset + i] - (u[i] * x + v[i] * y)
                return top, low

            for later in cols[k + 2 :]:
                eliminate(later, q)
            top, low = eliminate(strips, first + q)
            ra = lax.rsqrt(a)
            rows += [top * ra, (a * low - b * top) * (ra * lax.rsqrt(det))]
    out = []
    for s in range(0, size, 8):
        strip = rows[s]
        for k in range(1, 8):
            strip = jnp.where(place == k, rows[s + k], strip)
        out.append(strip)
    return jnp.concatenate(out, axis=0)[:, size:]


def refine_kernel(scale, side_ref, kept_ref, other_ref, start_ref, table_ref, basis_ref):
    kept, other = kept_ref[...], other_ref[...]
    low = side_ref[0] == 0
    both = [jnp.where(low, kept, other), jnp.where(low, other, kept)]
    blocks = jnp.concatenate(both, axis=0) * scale
    size = blocks.shape[1] // 2
    b00, b10, b20 = (blocks[i * size : (i + 1) * size, :size] for i in range(3))
    b11, b21, b22 = (blocks[i * size : (i + 1) * size, size:] for i in range(3))
    core = jnp.concatenate(
        [
            jnp.concatenate([b00, b10.T, b20.T], axis=1),
            jnp.concatenate([b10, b11, b21.T], axis=1),
            jnp.concatenate([b20, b21, b22], axis=1),
        ],
        axis=0,
    )
    wide = table_ref[...].astype(jnp.float32)
    panel = exact_dot_t(exact_dot(start_ref[...], core), wide)
    gram = exact_dot_t(exact_dot(wide, core), wide)
    for sweep in range(ITERS):
        inverse = inverse_factor(exact_dot_t(panel, panel))
        if sweep < ITERS - 1:
            panel = exact_dot(inverse, exact_dot(panel, gram))
    basis_ref[...] = exact_dot(inverse, panel).astype(jnp.bfloat16)


def refine(side, kept, other, start, table, scale):
    vmem = pl.BlockSpec(memory_space=pltpu.VMEM)
    return pl.pallas_call(
        functools.partial(refine_kernel, scale),
        out_shape=jax.ShapeDtypeStruct((start.shape[0], table.shape[0]), jnp.bfloat16),
        in_specs=[pl.BlockSpec(memory_space=pltpu.SMEM)] + [vmem] * 4,
        out_specs=vmem,
        compiler_params=pltpu.CompilerParams(vmem_limit_bytes=32 * 2**20),
        name="refine",
    )(side, kept, other, start, table)


def body(flux_east, flux_north, band_freqs, start_basis):
    hour_count, row_count, col_count = flux_east.shape
    tile_count = lax.axis_size("tile")
    cell_total = row_count * col_count * tile_count
    scale = (2.0 / hour_count) ** 2 / cell_total
    before, after = halo_rows(flux_east, "tile")
    table = wave_table(band_freqs, hour_count)
    start = exact_dot(start_basis.T, table.astype(jnp.float32))
    padded = jnp.concatenate([before, flux_east, after], axis=1)
    northward = jnp.pad(flux_north.astype(jnp.float32), ((0, 0), (0, 0), (1, 1)))
    across = 0.5 * (northward[:, :, 2:] - northward[:, :, :-2])
    eastward = padded.astype(jnp.float32)
    along = 0.5 * (eastward[:, 2:, :] - eastward[:, :-2, :])
    convergence = (along + across).astype(jnp.bfloat16).reshape(hour_count, row_count * col_count)
    bands = jnp.dot(table.T, convergence, preferred_element_type=jnp.float32).astype(jnp.bfloat16)
    filtered = (
        jnp.dot(table, bands, preferred_element_type=jnp.float32) * (2.0 / hour_count)
    ).astype(jnp.bfloat16)
    core = jnp.dot(bands, bands.T, preferred_element_type=jnp.float32)
    kept, other = summed_halves(packed(core), "tile")
    side = (lax.axis_index("tile") % 2).astype(jnp.int32).reshape(1)
    basis_t = refine(side, kept, other, start, table, scale)
    coefficients = jnp.dot(basis_t, filtered, preferred_element_type=jnp.float32).astype(
        jnp.bfloat16
    )
    rebuilt = jnp.dot(basis_t.T, coefficients, preferred_element_type=jnp.float32).astype(
        jnp.bfloat16
    )
    return rebuilt.reshape(hour_count, row_count, col_count)


def solution(mesh):
    placed = (P(None, ("grp", "tile"), None), P(None, ("grp", "tile"), None), P(), P())
    return jax.shard_map(
        body, mesh=mesh, in_specs=placed, out_specs=P(None, ("grp", "tile"), None), check_vma=False
    )
```

time: 178 us -> 45.8 us (0.26)
  waiting for transfers between devices: 93.5 us -> 9.39 us
  other arithmetic: 53.3 us -> 9.66 us
  between operations: 13.7 us -> 0.19 us
  Pallas kernels: 0 us -> 9.42 us
  starting transfers between devices: 4.46 us -> 11.2 us
  matrix products: 9.48 us -> 2.79 us
    psum x1 -> x0, waiting for transfers between devices: 93.4 us -> none  [body(): gram = lax.psum(local_gram, 'tile') * factor_scale]
    another operation x21 -> x1, other arithmetic: 48.8 us -> 0.54 us  [the longest x12 26.1 us: orthonormal(): factor = jnp.linalg.cholesky(crossed)]
    pallas_call x0 -> x1, Pallas kernels: none -> 9.42 us  [refine(): pl.pallas_call(functools.partial(refine_kernel, scale), out_shape=jax.Sha...]
    ppermute x2 -> x7, waiting for transfers between devices: 0.01 us -> 9.39 us  [the longest x3 7.17 us: summed_halves(): kept = kept + lax.ppermute(kept, axis, partners(count, mask))]
    ppermute x2 -> x7, starting transfers between devices: 4.46 us -> 11.2 us  [the longest x3 5.89 us: summed_halves(): kept = kept + lax.ppermute(kept, axis, partners(count, mask))]
    dot_general x13 -> x4, matrix products: 7.81 us -> 2.21 us  [the longest x1 0.85 us: body(): jnp.dot(basis_t, filtered, preferred_element_type=jnp.float32)]
    pad x1, other arithmetic: 2.3 us -> 4.95 us  [body(): jnp.pad(flux_north.astype(jnp.float32), ((0, 0), (0, 0), (1, 1)))]
    select_n x0 -> x2, other arithmetic: none -> 1.8 us  [the longest x1 1.52 us: halo_rows(): jnp.where(even, head, tail)]
  transfers between devices with their start and end apart: 3 -> 7, of which waited for: 1 -> 5; matrix products, arithmetic and copies ran while one was open for 2% -> 13% of each run, Pallas kernels for 0% -> 0%
where the time goes in v1:
time: 45.8 us; the launch traced here: 45.6 us
  starting transfers between devices  11.2 us (24%)
  other arithmetic  9.66 us (21%)
  Pallas kernels  9.42 us (21%)
  waiting for transfers between devices  9.39 us (21%)
  local copies, waits for them, and re-layouts  2.97 us (6%)
  matrix products  2.79 us (6%)
    pallas_call x1, Pallas kernels, refine(): pl.pallas_call(functools.partial(refine_kernel, scale), out_shape=jax.Sha...  9.42 us
    ppermute x3, waiting for transfers between devices, summed_halves(): kept = kept + lax.ppermute(kept, axis, partners(count, mask))  7.17 us
    ppermute x3, starting transfers between devices, summed_halves(): kept = kept + lax.ppermute(kept, axis, partners(count, mask))  5.89 us
    pad x1, other arithmetic, body(): jnp.pad(flux_north.astype(jnp.float32), ((0, 0), (0, 0), (1, 1)))  4.95 us
    ppermute x1, starting transfers between devices, halo_rows(): lax.ppermute(jnp.where(even, tail, head), axis, inner + [(j, i) for i, j...  4.36 us
    unnamed x9, local copies, waits for them, and re-layouts  2.87 us
    select_n x1, other arithmetic, halo_rows(): jnp.where(even, head, tail)  1.52 us
    ppermute x1, waiting for transfers between devices, summed_halves(): kept = kept + lax.ppermute(given, axis, partners(count, 1))  1.11 us
  transfers between devices with their start and end apart: 7, of which 5 were waited for; matrix products, arithmetic and copies ran while one was open for 13% of the time, Pallas kernels for 0%

profile of v1, /device:TPU:0, one launch (start us, length us, event | category | flops | bytes accessed | tf_op | source)
XLA Modules:
  0.0 45.6 jit_solution(18280563857224558758)
XLA Ops:
  0.0 1.5 %broadcast_select_fusion.3 = (bf16[256,1,128]{2,1,0:T(2,128)(2,1)S(1)}, bf16[256,1,128]{2,1,0:T(2,128)(2,1)S(1)}) fusion(pred[]{:T(512)S(6)} %eq.9, bf16[256,24,128]{2,1,0:T(8,128)(2,1)} %param.4), kind=kLoop, calls=%fused_computation.19 | loop fusion | flops 65536 | bytes 262145 | tf_op jit(solution)/shard_map/jit(_where)/select_n | solution.py:27
  1.5 0.7 %collective-permute-start = (bf16[256,1,128]{2,1,0:T(2,128)(2,1)S(1)}, bf16[256,1,128]{2,1,0:T(2,128)(2,1)S(1)}, u32[]{:S(2)}, u32[]{:S(2)}) collective-permute-start(bf16[256,1,128]{2,1,0:T(2,128)(2,1)S(1)} %get-tuple-element.5), channel_id=1, source_target_pairs={{1,2},{3,4},{5,6},{7,8},{9,10},{11,12},{13,14},{2,1},{4,3},{6,5},{... | collective-permute-start | bytes 196616 | tf_op jit(solution)/shard_map/ppermute | solution.py:26
  2.2 4.4 %collective-permute-start.1 = (bf16[256,1,128]{2,1,0:T(2,128)(2,1)S(1)}, bf16[256,1,128]{2,1,0:T(2,128)(2,1)S(1)}, u32[]{:S(2)}, u32[]{:S(2)}) collective-permute-start(bf16[256,1,128]{2,1,0:T(2,128)(2,1)S(1)} %get-tuple-element.6), channel_id=1, source_target_pairs={{0,1},{2,3},{4,5},{6,7},{8,9},{10,11},{12,13},{14,15},{1,0},{3,2},... | collective-permute-start | bytes 196616 | tf_op jit(solution)/shard_map/ppermute | solution.py:29
  6.6 5.0 %pad_convert_fusion = f32[256,24,130]{2,1,0:T(8,128)} fusion(bf16[256,24,128]{2,1,0:T(8,128)(2,1)} %param.5), kind=kLoop, calls=%fused_computation.10 | loop fusion | flops 798720 | bytes 4767744 | tf_op jit(solution)/shard_map/jit(_pad)/pad | solution.py:178
  11.5 0.5 %cosine_convert_fusion = (bf16[256,96]{1,0:T(8,128)(2,1)S(1)}, bf16[256,96]{1,0:T(8,128)(2,1)S(1)}) fusion(s32[96]{0:T(128)S(1)} %copy-done.3), kind=kLoop, calls=%fused_computation.28 | loop fusion | flops 393216 | bytes 98688 | tf_op jit(solution)/shard_map/convert.2
  12.1 0.3 broadcast_select_fusion.1
  12.4 1.1 %maximum_convert_fusion = f32[256,26,128]{2,1,0:T(8,128)S(1)} fusion(bf16[256,1,128]{2,1,0:T(2,128)(2,1)S(1)} %get-tuple-element.8, bf16[256,24,128]{2,1,0:T(8,128)(2,1)S(1)} %copy-done.2, bf16[256,1,128]{2,1,0:T(2,128)(2,1)S(1)} %get-tuple-element.7), kind=kLoop, calls=%fused_computation.11 | loop fusion | flops 5111808 | bytes 5111808 | tf_op jit(solution)/shard_map/convert_element_type | solution.py:180
  13.5 1.4 %copy-done.1 = f32[256,24,130]{2,1,0:T(8,128)S(1)} copy-done((f32[256,24,130]{2,1,0:T(8,128)S(1)}, f32[256,24,130]{2,1,0:T(8,128)}, u32[]{:S(2)}) %copy-start.1) | copy-done | bytes 3194904
  14.9 1.1 %fusion.3 = bf16[256,24,128]{2,1,0:T(8,128)(2,1)S(1)} fusion(f32[256,24,130]{2,1,0:T(8,128)S(1)} %copy-done.1, f32[256,26,128]{2,1,0:T(8,128)S(1)} %maximum_convert_fusion), kind=kLoop, calls=%fused_computation.8 | loop fusion | flops 3932160 | bytes 14155776 | tf_op jit(solution)/shard_map/convert_element_type | solution.py:182
  16.0 0.6 %convolution_convert_fusion.1 = bf16[192,3072]{1,0:T(8,128)(2,1)S(1)} fusion(bf16[32,8,24,128]{3,2,1,0:T(8,128)(2,1)S(1)} %bitcast.17, bf16[256,96]{1,0:T(8,128)(2,1)S(1)} %get-tuple-element.10, bf16[256,96]{1,0:T(8,128)(2,1)S(1)} %get-tuple-element.9), kind=kOutput, calls=%fused_computation.3 | convolution fusion | flops 302776320 | bytes 2850816 | tf_op jit(solution)/shard_map/dot_general | solution.py:183
  16.6 0.5 %fusion.14 = f32[192,192]{1,0:T(8,128)S(1)} fusion(bf16[192,3072]{1,0:T(8,128)(2,1)S(1)} %convolution_convert_fusion.1), kind=kOutput, calls=%fused_computation.36 | convolution fusion | flops 226492416 | bytes 1327104 | tf_op jit(solution)/shard_map/dot_general | solution.py:187
  17.5 1.1 %collective-permute-done.2 = f32[96,128]{1,0:T(8,128)S(1)} collective-permute-done((f32[96,128]{1,0:T(8,128)S(1)}, f32[96,128]{1,0:T(8,128)S(1)}, u32[]{:S(2)}, u32[]{:S(2)}) %collective-permute-start.2) | collective-permute-done | bytes 49184 | tf_op jit(solution)/shard_map/ppermute | solution.py:56
  18.6 1.6 %collective-permute-start.3 = (f32[96,128]{1,0:T(8,128)S(1)}, f32[96,128]{1,0:T(8,128)S(1)}, u32[]{:S(2)}, u32[]{:S(2)}) collective-permute-start(f32[96,128]{1,0:T(8,128)S(1)} %dynamic-slice_add_fusion), channel_id=1, source_target_pairs={{0,2},{1,3},{2,0},{3,1},{4,6},{5,7},{6,4},{7,5},{8,10},{9,11},{10,... | collective-permute-start | bytes 147464 | tf_op jit(solution)/shard_map/ppermute | solution.py:59
  20.2 2.5 %collective-permute-done.3 = f32[96,128]{1,0:T(8,128)S(1)} collective-permute-done((f32[96,128]{1,0:T(8,128)S(1)}, f32[96,128]{1,0:T(8,128)S(1)}, u32[]{:S(2)}, u32[]{:S(2)}) %collective-permute-start.3) | collective-permute-done | bytes 49184 | tf_op jit(solution)/shard_map/ppermute | solution.py:59
  22.7 1.6 %collective-permute-start.4 = (f32[96,128]{1,0:T(8,128)S(1)}, f32[96,128]{1,0:T(8,128)S(1)}, u32[]{:S(2)}, u32[]{:S(2)}) collective-permute-start(f32[96,128]{1,0:T(8,128)S(1)} %add.42), channel_id=1, source_target_pairs={{0,4},{1,5},{2,6},{3,7},{4,0},{5,1},{6,2},{7,3},{8,12},{9,13},{10,... | collective-permute-start | bytes 147464 | tf_op jit(solution)/shard_map/ppermute | solution.py:59
  24.4 2.5 %collective-permute-done.4 = f32[96,128]{1,0:T(8,128)S(1)} collective-permute-done((f32[96,128]{1,0:T(8,128)S(1)}, f32[96,128]{1,0:T(8,128)S(1)}, u32[]{:S(2)}, u32[]{:S(2)}) %collective-permute-start.4) | collective-permute-done | bytes 49184 | tf_op jit(solution)/shard_map/ppermute | solution.py:59
  26.9 2.6 %collective-permute-start.5 = (f32[96,128]{1,0:T(8,128)S(1)}, f32[96,128]{1,0:T(8,128)S(1)}, u32[]{:S(2)}, u32[]{:S(2)}) collective-permute-start(f32[96,128]{1,0:T(8,128)S(1)} %add.43), channel_id=1, source_target_pairs={{0,8},{1,9},{2,10},{3,11},{4,12},{5,13},{6,14},{7,15},{8,0},{9,1},... | collective-permute-start | bytes 147464 | tf_op jit(solution)/shard_map/ppermute | solution.py:59
  29.6 0.3 convolution_bitcast_fusion.start_ref
  29.8 2.1 %collective-permute-done.5 = f32[96,128]{1,0:T(8,128)S(1)} collective-permute-done((f32[96,128]{1,0:T(8,128)S(1)}, f32[96,128]{1,0:T(8,128)S(1)}, u32[]{:S(2)}, u32[]{:S(2)}) %collective-permute-start.5) | collective-permute-done | bytes 49184 | tf_op jit(solution)/shard_map/ppermute | solution.py:59
  32.2 1.1 %collective-permute-done.6.other_ref = f32[96,128]{1,0:T(8,128)S(1)} collective-permute-done((f32[96,128]{1,0:T(8,128)S(1)}, f32[96,128]{1,0:T(8,128)S(1)}, u32[]{:S(2)}, u32[]{:S(2)}) %collective-permute-start.6) | collective-permute-done | bytes 49184 | tf_op jit(solution)/shard_map/ppermute | solution.py:61
  33.3 9.4 %refine.1 = bf16[64,256]{1,0:T(8,128)(2,1)S(1)} custom-call(s32[1]{0:T(128)} %bitcast.side_ref, f32[96,128]{1,0:T(8,128)S(1)} %add.44.kept_ref, f32[96,128]{1,0:T(8,128)S(1)} %collective-permute-done.6.other_ref, f32[64,192]{1,0:T(8,128)S(1)} %convolution_bitcast_fusion.start_ref, bf16[256,192]{1,0:T(8,128)(2,1)S(1)} %pad_maximum_fusion.table_ref), custom_call_target="tpu_custom_call" | custom-call | tf_op jit(solution)/shard_map/refine/pallas_call | solution.py:159
  42.7 0.8 %convolution_convert_fusion.2 = bf16[64,3072]{1,0:T(8,128)(2,1)S(1)} fusion(bf16[64,256]{1,0:T(8,128)(2,1)S(1)} %refine.1, bf16[192,3072]{1,0:T(8,128)(2,1)S(1)} %convolution_convert_fusion.1, bf16[256,96]{1,0:T(8,128)(2,1)S(1)} %get-tuple-element.10, bf16[256,96]{1,0:T(8,128)(2,1)S(1)} %get-tuple-element.9), kind=kOutput, calls=%fused_computation.4 | convolution fusion | flops 404619264 | bytes 1703936 | tf_op jit(solution)/shard_map/dot_general | solution.py:191
  43.5 0.6 %fusion.6 = bf16[32,8,24,128]{3,1,2,0:T(8,128)(2,1)S(1)} fusion(bf16[64,256]{1,0:T(8,128)(2,1)S(1)} %refine.1, bf16[64,3072]{1,0:T(8,128)(2,1)S(1)} %convolution_convert_fusion.2), kind=kOutput, calls=%fused_computation.14 | convolution fusion | flops 101449728 | bytes 1998848 | tf_op jit(solution)/shard_map/dot_general | solution.py:194
  44.1 1.5 %copy.10 = bf16[32,8,24,128]{3,2,1,0:T(8,128)(2,1)} copy(bf16[32,8,24,128]{3,1,2,0:T(8,128)(2,1)S(1)} %fusion.6) | data formatting | bytes 3145728
  (21 shorter events, 0.6 us)
Async XLA Ops:
  0.0 29.6 %copy-start = (f32[256,64]{0,1:T(8,128)S(1)}, f32[256,64]{0,1:T(8,128)}, u32[]{:S(2)}) copy-start(f32[256,64]{0,1:T(8,128)} %param.7) | copy-start | bytes 196612
  1.5 10.6 %collective-permute-start = (bf16[256,1,128]{2,1,0:T(2,128)(2,1)S(1)}, bf16[256,1,128]{2,1,0:T(2,128)(2,1)S(1)}, u32[]{:S(2)}, u32[]{:S(2)}) collective-permute-start(bf16[256,1,128]{2,1,0:T(2,128)(2,1)S(1)} %get-tuple-element.5), channel_id=1, source_target_pairs={{1,2},{3,4},{5,6},{7,8},{9,10},{11,12},{13,14},{2,1},{4,3},{6,5},{... | collective-permute-start | bytes 196616 | tf_op jit(solution)/shard_map/ppermute | solution.py:26
  2.2 9.3 %copy-start.3 = (s32[96]{0:T(128)S(1)}, s32[96]{0:T(128)}, u32[]{:S(2)}) copy-start(s32[96]{0:T(128)} %param.6) | copy-start | bytes 1156
  2.2 10.2 %copy-start.2 = (bf16[256,24,128]{2,1,0:T(8,128)(2,1)S(1)}, bf16[256,24,128]{2,1,0:T(8,128)(2,1)}, u32[]{:S(2)}) copy-start(bf16[256,24,128]{2,1,0:T(8,128)(2,1)} %param.4) | copy-start | bytes 4718596
  2.2 9.9 %collective-permute-start.1 = (bf16[256,1,128]{2,1,0:T(2,128)(2,1)S(1)}, bf16[256,1,128]{2,1,0:T(2,128)(2,1)S(1)}, u32[]{:S(2)}, u32[]{:S(2)}) collective-permute-start(bf16[256,1,128]{2,1,0:T(2,128)(2,1)S(1)} %get-tuple-element.6), channel_id=1, source_target_pairs={{0,1},{2,3},{4,5},{6,7},{8,9},{10,11},{12,13},{14,15},{1,0},{3,2},... | collective-permute-start | bytes 196616 | tf_op jit(solution)/shard_map/ppermute | solution.py:29
  12.1 2.8 %copy-start.1 = (f32[256,24,130]{2,1,0:T(8,128)S(1)}, f32[256,24,130]{2,1,0:T(8,128)}, u32[]{:S(2)}) copy-start(f32[256,24,130]{2,1,0:T(8,128)} %pad_convert_fusion) | copy-start | bytes 9584644
  17.3 1.3 %collective-permute-start.2 = (f32[96,128]{1,0:T(8,128)S(1)}, f32[96,128]{1,0:T(8,128)S(1)}, u32[]{:S(2)}, u32[]{:S(2)}) collective-permute-start(f32[96,128]{1,0:T(8,128)S(1)} %constant_dynamic-slice_fusion), channel_id=1, source_target_pairs={{0,1},{1,0},{2,3},{3,2},{4,5},{5,4},{6,7},{7,6},{8,9},{9,8},{10,11... | collective-permute-start | bytes 147464 | tf_op jit(solution)/shard_map/ppermute | solution.py:56
  18.6 4.2 %collective-permute-start.3 = (f32[96,128]{1,0:T(8,128)S(1)}, f32[96,128]{1,0:T(8,128)S(1)}, u32[]{:S(2)}, u32[]{:S(2)}) collective-permute-start(f32[96,128]{1,0:T(8,128)S(1)} %dynamic-slice_add_fusion), channel_id=1, source_target_pairs={{0,2},{1,3},{2,0},{3,1},{4,6},{5,7},{6,4},{7,5},{8,10},{9,11},{10,... | collective-permute-start | bytes 147464 | tf_op jit(solution)/shard_map/ppermute | solution.py:59
  22.7 4.2 %collective-permute-start.4 = (f32[96,128]{1,0:T(8,128)S(1)}, f32[96,128]{1,0:T(8,128)S(1)}, u32[]{:S(2)}, u32[]{:S(2)}) collective-permute-start(f32[96,128]{1,0:T(8,128)S(1)} %add.42), channel_id=1, source_target_pairs={{0,4},{1,5},{2,6},{3,7},{4,0},{5,1},{6,2},{7,3},{8,12},{9,13},{10,... | collective-permute-start | bytes 147464 | tf_op jit(solution)/shard_map/ppermute | solution.py:59
  26.9 5.0 %collective-permute-start.5 = (f32[96,128]{1,0:T(8,128)S(1)}, f32[96,128]{1,0:T(8,128)S(1)}, u32[]{:S(2)}, u32[]{:S(2)}) collective-permute-start(f32[96,128]{1,0:T(8,128)S(1)} %add.43), channel_id=1, source_target_pairs={{0,8},{1,9},{2,10},{3,11},{4,12},{5,13},{6,14},{7,15},{8,0},{9,1},... | collective-permute-start | bytes 147464 | tf_op jit(solution)/shard_map/ppermute | solution.py:59
  32.0 1.3 %collective-permute-start.6 = (f32[96,128]{1,0:T(8,128)S(1)}, f32[96,128]{1,0:T(8,128)S(1)}, u32[]{:S(2)}, u32[]{:S(2)}) collective-permute-start(f32[96,128]{1,0:T(8,128)S(1)} %add.44.kept_ref), channel_id=1, source_target_pairs={{0,1},{1,0},{2,3},{3,2},{4,5},{5,4},{6,7},{7,6},{8,9},{9,8},{10,11... | collective-permute-start | bytes 147464 | tf_op jit(solution)/shard_map/ppermute | solution.py:61

commit v2 on v1

v2 whole, which is shorter than its diff:
```python
import functools
import math

import jax
import jax.numpy as jnp
from jax import lax
from jax.experimental import pallas as pl
from jax.experimental.pallas import tpu as pltpu
from jax.sharding import PartitionSpec as P

ITERS = 4
WIDE = 16
IN_STEPS = 4
OUT_STEPS = 4
INNER_MIB = 60
EXACT = lax.Precision.HIGHEST
VMEM = pl.BlockSpec(memory_space=pltpu.VMEM)
HBM = pl.BlockSpec(memory_space=pltpu.HBM)
MIB = 2**20


def partners(count, mask):
    return [(i, i ^ mask) for i in range(count)]


def parity(index, count):
    bits = index
    shift = 1
    while 1 << shift < count:
        bits = bits ^ (index >> shift)
        shift += 1
    return bits & 1


def wave_table(freqs, hour_count):
    shape = (hour_count, freqs.shape[1])
    times = lax.broadcasted_iota(jnp.int32, shape, 0)
    column = lax.broadcasted_iota(jnp.int32, shape, 1)
    quarter = hour_count // 4
    phase = times * freqs - jnp.where(column < shape[1] // 2, 0, quarter)
    phase = ((phase + 2 * quarter) & (hour_count - 1)) - 2 * quarter
    angle = (quarter - jnp.abs(phase)).astype(jnp.float32) * (2.0 * math.pi / hour_count)
    square = angle * angle
    series = 1.0
    for n in (13, 11, 9, 7, 5, 3):
        series = 1.0 - square * (1.0 / (n * (n - 1))) * series
    return angle * series


def dot(a, b):
    return lax.dot_general(a, b, (((1,), (0,)), ((), ())), preferred_element_type=jnp.float32)


def dot_t(a, b):
    return lax.dot_general(a, b, (((1,), (1,)), ((), ())), preferred_element_type=jnp.float32)


def exact_dot(a, b):
    return lax.dot_general(
        a, b, (((1,), (0,)), ((), ())), precision=EXACT, preferred_element_type=jnp.float32
    )


def exact_dot_t(a, b):
    return lax.dot_general(
        a, b, (((1,), (1,)), ((), ())), precision=EXACT, preferred_element_type=jnp.float32
    )


def cross_band(cols):
    ids = [lax.broadcasted_iota(jnp.int32, (cols, cols), d) for d in range(2)]
    band = jnp.where(ids[0] == ids[1] + 1, 0.5, jnp.where(ids[0] == ids[1] - 1, -0.5, 0.0))
    return band.astype(jnp.bfloat16)


def inner_kernel(
    freqs_ref,
    east_hbm,
    north_hbm,
    bands_ref,
    core_ref,
    edge_ref,
    near_ref,
    far_ref,
    table_ref,
    waves_ref,
    east_ref,
    north_ref,
    along_ref,
    across_ref,
    sems,
):
    hour_count, row_count, cols = east_ref.shape
    steps = sems.shape[0]
    hours = hour_count // steps
    flat = hours * row_count

    def copies(step):
        part = slice(step * hours, (step + 1) * hours)
        return [
            pltpu.make_async_copy(src.at[part], dst.at[part], sems.at[step, k])
            for k, (src, dst) in enumerate(((east_hbm, east_ref), (north_hbm, north_ref)))
        ]

    for step in range(steps):
        for copy in copies(step):
            copy.start()
    freqs = freqs_ref[...]
    table = wave_table(jnp.concatenate([freqs, freqs], axis=1), hour_count)
    waves = table.T.astype(jnp.bfloat16)
    table_ref[...] = table.astype(jnp.bfloat16)
    waves_ref[...] = waves
    band = cross_band(cols)
    for step in range(steps):
        for copy in copies(step):
            copy.wait()
        part = slice(step * hours, (step + 1) * hours)
        to = slice(step * flat, (step + 1) * flat)
        along_ref[to] = 0.5 * east_ref[part].astype(jnp.float32).reshape(flat, cols)
        north = north_ref[part].astype(jnp.float32).reshape(flat, cols).astype(jnp.bfloat16)
        across_ref[to] = dot(north, band)

    def at(ref, i):
        return ref[pl.ds(i, hour_count, stride=row_count)]

    head, tail = at(along_ref, 0) * 2.0, at(along_ref, row_count - 1) * 2.0
    even = lax.axis_index("tile") % 2 == 0
    near_ref[...] = jnp.where(even, tail, head).astype(jnp.bfloat16)
    far_ref[...] = jnp.where(even, head, tail).astype(jnp.bfloat16)
    edge_ref[:, :cols] = at(across_ref, 0) + at(along_ref, 1)
    edge_ref[:, cols:] = at(across_ref, row_count - 1) - at(along_ref, row_count - 2)
    core = None
    for i in range(0, row_count - 2, 2):
        pair = [
            (at(across_ref, k) + (at(along_ref, k + 1) - at(along_ref, k - 1))).astype(jnp.bfloat16)
            for k in (i + 1, i + 2)
        ]
        bands = dot(waves, jnp.concatenate(pair, axis=1)).astype(jnp.bfloat16)
        bands_ref[:, i * cols : (i + 2) * cols] = bands
        product = dot_t(bands, bands)
        core = product if core is None else core + product
    core_ref[...] = core


def inner(freqs, east, north):
    hour_count, row_count, cols = east.shape
    count = 2 * freqs.shape[1]
    f32, bf16 = jnp.float32, jnp.bfloat16
    return pl.pallas_call(
        inner_kernel,
        out_shape=[
            jax.ShapeDtypeStruct((count, (row_count - 2) * cols), bf16),
            jax.ShapeDtypeStruct((count, count), f32),
            jax.ShapeDtypeStruct((hour_count, 2 * cols), f32),
            jax.ShapeDtypeStruct((hour_count, cols), bf16),
            jax.ShapeDtypeStruct((hour_count, cols), bf16),
            jax.ShapeDtypeStruct((hour_count, count), bf16),
            jax.ShapeDtypeStruct((count, hour_count), bf16),
        ],
        in_specs=[VMEM, HBM, HBM],
        out_specs=[VMEM] * 7,
        scratch_shapes=[
            pltpu.VMEM(east.shape, east.dtype),
            pltpu.VMEM(north.shape, north.dtype),
            pltpu.VMEM((hour_count * row_count, cols), f32),
            pltpu.VMEM((hour_count * row_count, cols), f32),
            pltpu.SemaphoreType.DMA((IN_STEPS, 2)),
        ],
        compiler_params=pltpu.CompilerParams(vmem_limit_bytes=INNER_MIB * MIB),
        name="inner",
    )(freqs, east, north)


def outer_kernel(
    tile_count, edge_ref, near_ref, far_ref, waves_ref, core_ref, bands_ref, kept_ref, given_ref
):
    cols = near_ref.shape[1]
    near, far = near_ref[...].astype(jnp.float32), far_ref[...].astype(jnp.float32)
    tile = lax.axis_index("tile")
    far = jnp.where((tile > 0) & (tile < tile_count - 1), far, 0.0)
    even = tile % 2 == 0
    first = edge_ref[:, :cols] - 0.5 * jnp.where(even, far, near)
    final = edge_ref[:, cols:] + 0.5 * jnp.where(even, near, far)
    pair = [first.astype(jnp.bfloat16), final.astype(jnp.bfloat16)]
    bands = dot(waves_ref[...], jnp.concatenate(pair, axis=1)).astype(jnp.bfloat16)
    bands_ref[...] = bands
    core = core_ref[...] + dot_t(bands, bands)
    size = core.shape[0] // 3
    right = jnp.concatenate([core[size:, size : 2 * size], core[2 * size :, 2 * size :]], axis=0)
    packed = jnp.concatenate([core[:, :size], right], axis=1)
    half = packed.shape[0] // 2
    low = parity(tile, tile_count) == 0
    kept_ref[...] = jnp.where(low, packed[:half], packed[half:])
    given_ref[...] = jnp.where(low, packed[half:], packed[:half])


def outer(tile_count, edge, near, far, waves, core):
    count = waves.shape[0]
    half = jax.ShapeDtypeStruct((count // 2, count // 3 * 2), jnp.float32)
    return pl.pallas_call(
        functools.partial(outer_kernel, tile_count),
        out_shape=[jax.ShapeDtypeStruct((count, edge.shape[1]), jnp.bfloat16), half, half],
        in_specs=[VMEM] * 5,
        out_specs=[VMEM] * 3,
        compiler_params=pltpu.CompilerParams(vmem_limit_bytes=16 * MIB),
        name="outer",
    )(edge, near, far, waves, core)


def summed(kept, given, axis, beside):
    count = lax.axis_size(axis)
    kept = kept + lax.ppermute(given, axis, partners(count, 1))
    mask, first = 2, True
    while mask < count:
        kept = kept + lax.ppermute(kept, axis, partners(count, mask + 1))
        if first:
            kept, *beside = lax.optimization_barrier((kept, *beside))
        mask, first = mask * 2, False
    return kept, lax.ppermute(kept, axis, partners(count, 1)), beside


def lane(v, j):
    return jnp.broadcast_to(v[:, j : j + 1], v.shape)


def row(v, k):
    return jnp.broadcast_to(v[k : k + 1, :], v.shape)


def assembled(rows, place):
    strips = []
    for s in range(0, len(rows), 8):
        strip = rows[s]
        for k in range(1, 8):
            strip = jnp.where(place == k, rows[s + k], strip)
        strips.append(strip)
    return jnp.concatenate(strips, axis=0)


def inverse_factor(crossed):
    size = crossed.shape[0]
    ids = [lax.broadcasted_iota(jnp.int32, (size, size), d) for d in range(2)]
    eye = (ids[0] == ids[1]).astype(jnp.float32)
    joined = jnp.concatenate([crossed, eye], axis=1)
    strips = [joined[s : s + 8] for s in range(0, size, 8)]
    place = lax.broadcasted_iota(jnp.int32, strips[0].shape, 0)
    out = []
    for start in range(0, size, WIDE):
        first, last = start // 8, min(size, start + 2 * WIDE) // 8
        cols = [[lane(s, start + k) for s in strips[first:last]] for k in range(WIDE)]
        rows = []
        for k in range(0, WIDE, 2):
            q, s = k // 8, k % 8
            a, b, c = row(cols[k][q], s), row(cols[k][q], s + 1), row(cols[k + 1][q], s + 1)
            det = a * c - b * b
            inv = pl.reciprocal(det, approx=True)
            below = place > s + 1
            u = [jnp.where(below, cols[k][q], 0.0)] + cols[k][q + 1 :]
            v = [jnp.where(below, cols[k + 1][q], 0.0)] + cols[k + 1][q + 1 :]
            x = [i * c - j * b for i, j in zip(u, v)]
            y = [j * a - i * b for i, j in zip(u, v)]

            def eliminate(target, offset):
                top, low = row(target[offset], s), row(target[offset], s + 1)
                top_inv, low_inv = top * inv, low * inv
                for i in range(len(x)):
                    target[offset + i] = (target[offset + i] - x[i] * top_inv) - y[i] * low_inv
                return top, low

            for later in cols[k + 2 :]:
                eliminate(later, q)
            top, low = eliminate(strips, first + q)
            ra = lax.rsqrt(a)
            rows += [top * ra, (a * low - b * top) * (ra * lax.rsqrt(det))]
        out.append(assembled(rows, place))
        if 8 * last < size:
            update = exact_dot(out[-1].T[8 * last : size], out[-1])
            for i in range(last, size // 8):
                strips[i] = strips[i] - update[8 * (i - last) : 8 * (i - last) + 8]
    return jnp.concatenate(out, axis=0)[:, size:]


def thirds(x):
    high = x.astype(jnp.bfloat16)
    rest = x - high.astype(jnp.float32)
    middle = rest.astype(jnp.bfloat16)
    return high, middle, (rest - middle.astype(jnp.float32)).astype(jnp.bfloat16)


def project_kernel(
    scale,
    tile_count,
    kept_ref,
    other_ref,
    start_ref,
    table_ref,
    waves_ref,
    inside_ref,
    edges_ref,
    out_hbm,
    flat_ref,
    out_ref,
    sems,
):
    hour_count, row_count, cols = out_ref.shape
    kept, other = kept_ref[...], other_ref[...]
    low = parity(lax.axis_index("tile"), tile_count) == 0
    blocks = jnp.concatenate([jnp.where(low, kept, other), jnp.where(low, other, kept)], axis=0)
    blocks = blocks * scale
    size = blocks.shape[1] // 2
    b00, b10, b20 = (blocks[i * size : (i + 1) * size, :size] for i in range(3))
    b11, b21, b22 = (blocks[i * size : (i + 1) * size, size:] for i in range(3))
    core = jnp.concatenate(
        [
            jnp.concatenate([b00, b10.T, b20.T], axis=1),
            jnp.concatenate([b10, b11, b21.T], axis=1),
            jnp.concatenate([b20, b21, b22], axis=1),
        ],
        axis=0,
    )
    ids = [lax.broadcasted_iota(jnp.int32, (size, size), d) for d in range(2)]
    trace = jnp.sum(jnp.where(ids[0] == ids[1], b00 + b11 + b22, 0.0), keepdims=True)
    unit = 1.0 / (trace * (hour_count / 2))
    waves = waves_ref[...]

    def by_waves(x):
        high, middle, rest = (dot(part, waves) for part in thirds(x))
        return high + (middle + rest)

    panel = by_waves(exact_dot(start_ref[...], core))
    crossed = exact_dot_t(panel, panel) * unit * unit
    panel = panel * unit
    table = table_ref[...]
    high, middle, rest = (dot(table, part) for part in thirds(by_waves(core)))
    gram = (high + (middle + rest)) * unit
    for sweep in range(ITERS):
        inverse = inverse_factor(crossed)
        if sweep < ITERS - 1:
            panel = exact_dot(inverse, exact_dot(panel, gram))
            crossed = exact_dot_t(panel, panel)
    basis_t = exact_dot(inverse, panel)
    basis = basis_t.T.astype(jnp.bfloat16)
    basis_t = basis_t.astype(jnp.bfloat16)
    parts = [(inside_ref[:, i * cols : (i + 2) * cols], i + 1, i + 2) for i in range(0, row_count - 2, 2)]
    parts.append((edges_ref[...], 0, row_count - 1))
    parts = [(dot(basis_t, part).astype(jnp.bfloat16), rows) for part, *rows in parts]
    steps = sems.shape[0]
    hours = hour_count // steps
    flat = hours * row_count
    copies = []
    for step in range(steps):
        part = slice(step * hours, (step + 1) * hours)
        for coefficients, rows in parts:
            rebuilt = dot(basis[part], coefficients)
            for k, i in enumerate(rows):
                to = pl.ds(step * flat + i, hours, stride=row_count)
                flat_ref[to] = rebuilt[:, k * cols : (k + 1) * cols]
        whole = flat_ref[step * flat : (step + 1) * flat]
        out_ref[part] = whole.reshape(hours, row_count, cols).astype(jnp.bfloat16)
        copies.append(pltpu.make_async_copy(out_ref.at[part], out_hbm.at[part], sems.at[step]))
        copies[-1].start()
    for copy in copies:
        copy.wait()


def project(kept, other, start, table, waves, inside, edges, scale, shape):
    hour_count, row_count, cols = shape
    return pl.pallas_call(
        functools.partial(project_kernel, scale, lax.axis_size("tile")),
        out_shape=jax.ShapeDtypeStruct(shape, jnp.bfloat16),
        in_specs=[VMEM] * 7,
        out_specs=HBM,
        scratch_shapes=[
            pltpu.VMEM((hour_count * row_count, cols), jnp.float32),
            pltpu.VMEM(shape, jnp.bfloat16),
            pltpu.SemaphoreType.DMA((OUT_STEPS,)),
        ],
        compiler_params=pltpu.CompilerParams(vmem_limit_bytes=16 * MIB),
        name="project",
    )(kept, other, start, table, waves, inside, edges)


def body(flux_east, flux_north, band_freqs, start_basis):
    hour_count, row_count, col_count = flux_east.shape
    tile_count = lax.axis_size("tile")
    cell_total = row_count * col_count * tile_count
    scale = (2.0 / hour_count) ** 2 / cell_total
    bands, core, edge, near, far, table, waves = inner(band_freqs[None], flux_east, flux_north)
    near = lax.ppermute(near, "tile", partners(tile_count, 1))
    ring = [(i, (i + (1 if i % 2 else -1)) % tile_count) for i in range(tile_count)]
    far = lax.ppermute(far, "tile", ring)
    start = start_basis.T / jnp.max(jnp.abs(start_basis.T), axis=1, keepdims=True)
    start = exact_dot_t(start, waves.astype(jnp.float32))
    edge_bands, kept, given = outer(tile_count, edge, near, far, waves, core)

    def filtered(part):
        product = jnp.dot(table, part, preferred_element_type=jnp.float32)
        return (product * (2.0 / hour_count)).astype(jnp.bfloat16)

    beside = [filtered(bands), filtered(edge_bands), start]
    kept, other, (inside, edges, start) = summed(kept, given, "tile", beside)
    shape = flux_east.shape
    return project(kept, other, start, table, waves, inside, edges, scale, shape)


def solution(mesh):
    placed = (P(None, ("grp", "tile"), None), P(None, ("grp", "tile"), None), P(), P())
    return jax.shard_map(
        body, mesh=mesh, in_specs=placed, out_specs=P(None, ("grp", "tile"), None), check_vma=False
    )
```

time: 45.8 us -> 40.8 us (0.89)
  other arithmetic: 9.66 us -> 0.13 us
  Pallas kernels: 9.42 us -> 16.2 us
  waiting for transfers between devices: 9.39 us -> 13.7 us
  starting transfers between devices: 11.2 us -> 8.12 us
  local copies, waits for them, and re-layouts: 2.97 us -> 0.02 us
  matrix products: 2.79 us -> 2.31 us
    pallas_call x1 -> x3, Pallas kernels: 9.42 us -> 16.2 us  [the longest x1 9.98 us: project(): pl.pallas_call(functools.partial(project_kernel, scale, lax.axis_size('ti...]
    pad x1 -> x0, other arithmetic: 4.95 us -> none  [body(): jnp.pad(flux_north.astype(jnp.float32), ((0, 0), (0, 0), (1, 1)))]
    ppermute x7, waiting for transfers between devices: 9.39 us -> 13.7 us  [the longest x3 11.5 us: summed(): kept = kept + lax.ppermute(kept, axis, partners(count, mask + 1))]
    ppermute x7, starting transfers between devices: 11.2 us -> 8.12 us  [the longest x1 5.64 us: body(): far = lax.ppermute(far, 'tile', ring)]
    unnamed x9 -> x10, local copies, waits for them, and re-layouts: 2.87 us -> 0.02 us
    convert_element_type x2 -> x0, other arithmetic: 2.14 us -> none  [the longest x1 1.09 us: body(): eastward = padded.astype(jnp.float32)]
    select_n x2 -> x0, other arithmetic: 1.8 us -> none  [the longest x1 1.52 us: halo_rows(): jnp.where(even, head, tail)]
    another operation x1 -> x0, other arithmetic: 0.54 us -> none
  transfers between devices with their start and end apart: 7 -> 7, of which waited for: 5 -> 6; matrix products, arithmetic and copies ran while one was open for 13% -> 6% of each run, Pallas kernels for 0% -> 0%
where the time goes in v2:
time: 40.8 us; the launch traced here: 40.6 us
  Pallas kernels  16.2 us (40%)
  waiting for transfers between devices  13.7 us (34%)
  starting transfers between devices  8.12 us (20%)
  matrix products  2.31 us (6%)
    ppermute x3, waiting for transfers between devices, summed(): kept = kept + lax.ppermute(kept, axis, partners(count, mask + 1))  11.5 us
    pallas_call x1, Pallas kernels, project(): pl.pallas_call(functools.partial(project_kernel, scale, lax.axis_size('ti...  9.98 us
    pallas_call x1, Pallas kernels, inner(): pl.pallas_call(inner_kernel, out_shape=[jax.ShapeDtypeStruct((count, (row...  5.73 us
    ppermute x1, starting transfers between devices, body(): far = lax.ppermute(far, 'tile', ring)  5.64 us
    dot_general x2, matrix products, filtered(): product = jnp.dot(table, part, preferred_element_type=jnp.float32)  2.04 us
    ppermute x3, starting transfers between devices, summed(): kept = kept + lax.ppermute(kept, axis, partners(count, mask + 1))  1.71 us
    ppermute x1, waiting for transfers between devices, summed(): return (kept, lax.ppermute(kept, axis, partners(count, 1)), beside)  1.12 us
    ppermute x1, waiting for transfers between devices, summed(): kept = kept + lax.ppermute(given, axis, partners(count, 1))  0.94 us
  transfers between devices with their start and end apart: 7, of which 6 were waited for; matrix products, arithmetic and copies ran while one was open for 6% of the time, Pallas kernels for 0%

profile of v2, /device:TPU:0, one launch (start us, length us, event | category | flops | bytes accessed | tf_op | source)
XLA Modules:
  0.0 40.6 jit_solution(3461456136778101123)
XLA Ops:
  0.0 5.7 %inner.1 = (bf16[192,2816]{1,0:T(8,128)(2,1)}, f32[192,192]{1,0:T(8,128)}, f32[256,256]{1,0:T(8,128)}, bf16[256,128]{1,0:T(8,128)(2,1)}, bf16[256,128]{1,0:T(8,1...) custom-call(s32[1,96]{1,0:T(1,128)} %bitcast.6, bf16[256,24,128]{2,1,0:T(8,128)(2,1)} %east_hbm.1, ...), custom_call_target="tpu_custom_call" | custom-call | tf_op jit(solution)/shard_map/inner/pallas_call | solution.py:149
  5.7 0.0 copy-start.4
  5.8 0.0 copy-start.1
  5.8 0.0 copy-start.2
  5.8 0.5 %collective-permute-start = (bf16[256,128]{1,0:T(8,128)(2,1)}, bf16[256,128]{1,0:T(8,128)(2,1)S(1)}, u32[]{:S(2)}, u32[]{:S(2)}) collective-permute-start(bf16[256,128]{1,0:T(8,128)(2,1)} %get-tuple-element.20), channel_id=1, source_target_pairs={{0,1},{1,0},{2,3},{3,2},{4,5},{5,4},{6,7},{7,6},{8,9},{9,8},{10,11... | collective-permute-start | bytes 196616 | tf_op jit(solution)/shard_map/ppermute | solution.py:389
  6.3 5.6 %collective-permute-start.1 = (bf16[256,128]{1,0:T(8,128)(2,1)}, bf16[256,128]{1,0:T(8,128)(2,1)S(1)}, u32[]{:S(2)}, u32[]{:S(2)}) collective-permute-start(bf16[256,128]{1,0:T(8,128)(2,1)} %get-tuple-element.21), channel_id=1, source_target_pairs={{0,15},{1,2},{2,1},{3,4},{4,3},{5,6},{6,5},{7,8},{8,7},{9,10},{10,... | collective-permute-start | bytes 196616 | tf_op jit(solution)/shard_map/ppermute | solution.py:391
  11.9 1.9 %fusion.inside_ref = bf16[256,2816]{1,0:T(8,128)(2,1)S(1)} fusion(bf16[256,192]{1,0:T(8,128)(2,1)} %get-tuple-element.26.table_ref, bf16[192,2816]{1,0:T(8,128)(2,1)} %get-tuple-element.27), kind=kOutput, calls=%fused_computation.1 | convolution fusion | flops 278265856 | bytes 2621440 | tf_op jit(solution)/shard_map/dot_general | solution.py:397
  13.8 0.1 abs_reduce_fusion
  13.9 0.0 collective-permute-done.near_ref
  13.9 0.2 collective-permute-done.1.far_ref
  14.2 0.4 %outer.1 = (bf16[192,256]{1,0:T(8,128)(2,1)S(1)}, f32[96,128]{1,0:T(8,128)S(1)}, f32[96,128]{1,0:T(8,128)S(1)}) custom-call(f32[256,256]{1,0:T(8,128)S(1)} %copy-done.2, bf16[256,128]{1,0:T(8,128)(2,1)S(1)} %collective-permute-done.near_ref, bf16[256,128]{1,0:T(8,128)(2,1)S(1)} %collective-permute-done.1.far_ref, bf16[192,256]{1,0:T(8,128)(2,1)S(1)} %copy-done.1, ...), custom_call_target="tpu_custom_call" | custom-call | tf_op jit(solution)/shard_map/outer/pallas_call | solution.py:200
  14.6 0.1 collective-permute-start.2
  14.7 0.3 fusion.2.start_ref
  15.0 0.9 %collective-permute-done.2 = f32[96,128]{1,0:T(8,128)S(1)} collective-permute-done((f32[96,128]{1,0:T(8,128)S(1)}, f32[96,128]{1,0:T(8,128)S(1)}, u32[]{:S(2)}, u32[]{:S(2)}) %collective-permute-start.2) | collective-permute-done | bytes 49184 | tf_op jit(solution)/shard_map/ppermute | solution.py:212
  15.9 0.1 collective-permute-start.3
  16.0 0.2 fusion.1.edges_ref
  16.2 3.6 %collective-permute-done.3 = f32[96,128]{1,0:T(8,128)S(1)} collective-permute-done((f32[96,128]{1,0:T(8,128)S(1)}, f32[96,128]{1,0:T(8,128)S(1)}, u32[]{:S(2)}, u32[]{:S(2)}) %collective-permute-start.3) | collective-permute-done | bytes 49184 | tf_op jit(solution)/shard_map/ppermute | solution.py:215
  19.8 0.1 collective-permute-start.4
  19.8 3.7 %collective-permute-done.4 = f32[96,128]{1,0:T(8,128)S(1)} collective-permute-done((f32[96,128]{1,0:T(8,128)S(1)}, f32[96,128]{1,0:T(8,128)S(1)}, u32[]{:S(2)}, u32[]{:S(2)}) %collective-permute-start.4) | collective-permute-done | bytes 49184 | tf_op jit(solution)/shard_map/ppermute | solution.py:215
  23.6 1.6 %collective-permute-start.5 = (f32[96,128]{1,0:T(8,128)S(1)}, f32[96,128]{1,0:T(8,128)S(1)}, u32[]{:S(2)}, u32[]{:S(2)}) collective-permute-start(f32[96,128]{1,0:T(8,128)S(1)} %add.14), channel_id=1, source_target_pairs={{0,9},{1,8},{2,11},{3,10},{4,13},{5,12},{6,15},{7,14},{8,1},{9,0},... | collective-permute-start | bytes 147464 | tf_op jit(solution)/shard_map/ppermute | solution.py:215
  25.2 4.2 %collective-permute-done.5 = f32[96,128]{1,0:T(8,128)S(1)} collective-permute-done((f32[96,128]{1,0:T(8,128)S(1)}, f32[96,128]{1,0:T(8,128)S(1)}, u32[]{:S(2)}, u32[]{:S(2)}) %collective-permute-start.5) | collective-permute-done | bytes 49184 | tf_op jit(solution)/shard_map/ppermute | solution.py:215
  29.3 0.2 collective-permute-start.6
  29.5 1.1 %collective-permute-done.6.other_ref = f32[96,128]{1,0:T(8,128)S(1)} collective-permute-done((f32[96,128]{1,0:T(8,128)S(1)}, f32[96,128]{1,0:T(8,128)S(1)}, u32[]{:S(2)}, u32[]{:S(2)}) %collective-permute-start.6) | collective-permute-done | bytes 49184 | tf_op jit(solution)/shard_map/ppermute | solution.py:219
  30.6 10.0 %project.1 = bf16[256,24,128]{2,1,0:T(8,128)(2,1)} custom-call(f32[96,128]{1,0:T(8,128)S(1)} %add.15.kept_ref, f32[96,128]{1,0:T(8,128)S(1)} %collective-permute-done.6.other_ref, f32[64,192]{1,0:T(8,128)S(1)} %fusion.2.start_ref, bf16[256,192]{1,0:T(8,128)(2,1)S(1)} %copy-done, bf16[192,256]{1,0:T(8,128)(2,1)S(1)} %copy-done.1, ...), custom_call_target="tpu_custom_call" | custom-call | tf_op jit(solution)/shard_map/project/pallas_call | solution.py:368
  (11 shorter events, 0.0 us)
Async XLA Ops:
  5.7 8.1 %copy-start.4 = (f32[256,64]{0,1:T(8,128)S(1)}, f32[256,64]{0,1:T(8,128)}, u32[]{:S(2)}) copy-start(f32[256,64]{0,1:T(8,128)} %param.7) | copy-start | bytes 196612
  5.8 8.4 %copy-start.1 = (bf16[192,256]{1,0:T(8,128)(2,1)S(1)}, bf16[192,256]{1,0:T(8,128)(2,1)}, u32[]{:S(2)}) copy-start(bf16[192,256]{1,0:T(8,128)(2,1)} %get-tuple-element.22.waves_ref) | copy-start | bytes 294916
  5.8 8.4 %copy-start.2 = (f32[256,256]{1,0:T(8,128)S(1)}, f32[256,256]{1,0:T(8,128)}, u32[]{:S(2)}) copy-start(f32[256,256]{1,0:T(8,128)} %get-tuple-element.19.edge_ref) | copy-start | bytes 786436
  5.8 8.4 %copy-start.3 = (f32[192,192]{1,0:T(8,128)S(1)}, f32[192,192]{1,0:T(8,128)}, u32[]{:S(2)}) copy-start(f32[192,192]{1,0:T(8,128)} %get-tuple-element.23.core_ref) | copy-start | bytes 442372
  5.8 8.2 %collective-permute-start = (bf16[256,128]{1,0:T(8,128)(2,1)}, bf16[256,128]{1,0:T(8,128)(2,1)S(1)}, u32[]{:S(2)}, u32[]{:S(2)}) collective-permute-start(bf16[256,128]{1,0:T(8,128)(2,1)} %get-tuple-element.20), channel_id=1, source_target_pairs={{0,1},{1,0},{2,3},{3,2},{4,5},{5,4},{6,7},{7,6},{8,9},{9,8},{10,11... | collective-permute-start | bytes 196616 | tf_op jit(solution)/shard_map/ppermute | solution.py:389
  6.3 7.9 %collective-permute-start.1 = (bf16[256,128]{1,0:T(8,128)(2,1)}, bf16[256,128]{1,0:T(8,128)(2,1)S(1)}, u32[]{:S(2)}, u32[]{:S(2)}) collective-permute-start(bf16[256,128]{1,0:T(8,128)(2,1)} %get-tuple-element.21), channel_id=1, source_target_pairs={{0,15},{1,2},{2,1},{3,4},{4,3},{5,6},{6,5},{7,8},{8,7},{9,10},{10,... | collective-permute-start | bytes 196616 | tf_op jit(solution)/shard_map/ppermute | solution.py:391
  11.9 4.1 %copy-start = (bf16[256,192]{1,0:T(8,128)(2,1)S(1)}, bf16[256,192]{1,0:T(8,128)(2,1)}, u32[]{:S(2)}) copy-start(bf16[256,192]{1,0:T(8,128)(2,1)} %get-tuple-element.26.table_ref) | copy-start | bytes 294916
  14.6 1.3 %collective-permute-start.2 = (f32[96,128]{1,0:T(8,128)S(1)}, f32[96,128]{1,0:T(8,128)S(1)}, u32[]{:S(2)}, u32[]{:S(2)}) collective-permute-start(f32[96,128]{1,0:T(8,128)S(1)} %get-tuple-element.25), channel_id=1, source_target_pairs={{0,1},{1,0},{2,3},{3,2},{4,5},{5,4},{6,7},{7,6},{8,9},{9,8},{10,11... | collective-permute-start | bytes 147464 | tf_op jit(solution)/shard_map/ppermute | solution.py:212
  15.9 3.8 %collective-permute-start.3 = (f32[96,128]{1,0:T(8,128)S(1)}, f32[96,128]{1,0:T(8,128)S(1)}, u32[]{:S(2)}, u32[]{:S(2)}) collective-permute-start(f32[96,128]{1,0:T(8,128)S(1)} %add.12), channel_id=1, source_target_pairs={{0,3},{1,2},{2,1},{3,0},{4,7},{5,6},{6,5},{7,4},{8,11},{9,10},{10,... | collective-permute-start | bytes 147464 | tf_op jit(solution)/shard_map/ppermute | solution.py:215
  19.8 3.8 %collective-permute-start.4 = (f32[96,128]{1,0:T(8,128)S(1)}, f32[96,128]{1,0:T(8,128)S(1)}, u32[]{:S(2)}, u32[]{:S(2)}) collective-permute-start(f32[96,128]{1,0:T(8,128)S(1)} %add.13), channel_id=1, source_target_pairs={{0,5},{1,4},{2,7},{3,6},{4,1},{5,0},{6,3},{7,2},{8,13},{9,12},{10,... | collective-permute-start | bytes 147464 | tf_op jit(solution)/shard_map/ppermute | solution.py:215
  23.6 5.8 %collective-permute-start.5 = (f32[96,128]{1,0:T(8,128)S(1)}, f32[96,128]{1,0:T(8,128)S(1)}, u32[]{:S(2)}, u32[]{:S(2)}) collective-permute-start(f32[96,128]{1,0:T(8,128)S(1)} %add.14), channel_id=1, source_target_pairs={{0,9},{1,8},{2,11},{3,10},{4,13},{5,12},{6,15},{7,14},{8,1},{9,0},... | collective-permute-start | bytes 147464 | tf_op jit(solution)/shard_map/ppermute | solution.py:215
  29.3 1.3 %collective-permute-start.6 = (f32[96,128]{1,0:T(8,128)S(1)}, f32[96,128]{1,0:T(8,128)S(1)}, u32[]{:S(2)}, u32[]{:S(2)}) collective-permute-start(f32[96,128]{1,0:T(8,128)S(1)} %add.15.kept_ref), channel_id=1, source_target_pairs={{0,1},{1,0},{2,3},{3,2},{4,5},{5,4},{6,7},{7,6},{8,9},{9,8},{10,11... | collective-permute-start | bytes 147464 | tf_op jit(solution)/shard_map/ppermute | solution.py:219

commit v3 on v2

--- a/solution.py
+++ b/solution.py
@@ -12,7 +12,7 @@
 WIDE = 16
 IN_STEPS = 4
 OUT_STEPS = 4
-INNER_MIB = 60
+CONVERGE_KIB = 52736
 EXACT = lax.Precision.HIGHEST
 VMEM = pl.BlockSpec(memory_space=pltpu.VMEM)
 HBM = pl.BlockSpec(memory_space=pltpu.HBM)
@@ -21,6 +21,14 @@
 
 def partners(count, mask):
     return [(i, i ^ mask) for i in range(count)]
+
+
+def across_pairs(count, first):
+    to = [i ^ 1 for i in range(count)]
+    for i in range(2 * first, count - 3, 4):
+        for j in range(2):
+            to[i + j], to[i + 3 - j] = i + 3 - j, i + j
+    return list(enumerate(to))
 
 
 def parity(index, count):
@@ -73,17 +81,13 @@
     return band.astype(jnp.bfloat16)
 
 
-def inner_kernel(
-    freqs_ref,
+def converge_kernel(
     east_hbm,
     north_hbm,
-    bands_ref,
-    core_ref,
+    inner_ref,
     edge_ref,
     near_ref,
     far_ref,
-    table_ref,
-    waves_ref,
     east_ref,
     north_ref,
     along_ref,
@@ -94,71 +98,53 @@
     steps = sems.shape[0]
     hours = hour_count // steps
     flat = hours * row_count
-
-    def copies(step):
-        part = slice(step * hours, (step + 1) * hours)
-        return [
-            pltpu.make_async_copy(src.at[part], dst.at[part], sems.at[step, k])
-            for k, (src, dst) in enumerate(((east_hbm, east_ref), (north_hbm, north_ref)))
-        ]
-
-    for step in range(steps):
-        for copy in copies(step):
+    arrays = ((east_hbm, east_ref), (north_hbm, north_ref))
+    parts = [slice(step * hours, (step + 1) * hours) for step in range(steps)]
+    copies = [
+        [pltpu.make_async_copy(a.at[p], b.at[p], sems.at[i, k]) for k, (a, b) in enumerate(arrays)]
+        for i, p in enumerate(parts)
+    ]
+    for pair in copies:
+        for copy in pair:
             copy.start()
-    freqs = freqs_ref[...]
-    table = wave_table(jnp.concatenate([freqs, freqs], axis=1), hour_count)
-    waves = table.T.astype(jnp.bfloat16)
-    table_ref[...] = table.astype(jnp.bfloat16)
-    waves_ref[...] = waves
     band = cross_band(cols)
-    for step in range(steps):
-        for copy in copies(step):
+    for step, part in enumerate(parts):
+        for copy in copies[step]:
             copy.wait()
-        part = slice(step * hours, (step + 1) * hours)
         to = slice(step * flat, (step + 1) * flat)
         along_ref[to] = 0.5 * east_ref[part].astype(jnp.float32).reshape(flat, cols)
         north = north_ref[part].astype(jnp.float32).reshape(flat, cols).astype(jnp.bfloat16)
         across_ref[to] = dot(north, band)
 
-    def at(ref, i):
-        return ref[pl.ds(i, hour_count, stride=row_count)]
-
-    head, tail = at(along_ref, 0) * 2.0, at(along_ref, row_count - 1) * 2.0
-    even = lax.axis_index("tile") % 2 == 0
-    near_ref[...] = jnp.where(even, tail, head).astype(jnp.bfloat16)
-    far_ref[...] = jnp.where(even, head, tail).astype(jnp.bfloat16)
-    edge_ref[:, :cols] = at(across_ref, 0) + at(along_ref, 1)
-    edge_ref[:, cols:] = at(across_ref, row_count - 1) - at(along_ref, row_count - 2)
-    core = None
-    for i in range(0, row_count - 2, 2):
-        pair = [
-            (at(across_ref, k) + (at(along_ref, k + 1) - at(along_ref, k - 1))).astype(jnp.bfloat16)
-            for k in (i + 1, i + 2)
-        ]
-        bands = dot(waves, jnp.concatenate(pair, axis=1)).astype(jnp.bfloat16)
-        bands_ref[:, i * cols : (i + 2) * cols] = bands
-        product = dot_t(bands, bands)
-        core = product if core is None else core + product
-    core_ref[...] = core
-
-
-def inner(freqs, east, north):
+        def at(ref, i):
+            return ref[pl.ds(step * flat + i, hours, stride=row_count)]
+
+        head, tail = at(along_ref, 0) * 2.0, at(along_ref, row_count - 1) * 2.0
+        even = lax.axis_index("tile") % 2 == 0
+        near_ref[part] = jnp.where(even, tail, head).astype(jnp.bfloat16)
+        far_ref[part] = jnp.where(even, head, tail).astype(jnp.bfloat16)
+        edge_ref[part, :cols] = at(across_ref, 0) + at(along_ref, 1)
+        edge_ref[part, cols:] = at(across_ref, row_count - 1) - at(along_ref, row_count - 2)
+        for i in range(1, row_count - 1):
+            along = at(along_ref, i + 1) - at(along_ref, i - 1)
+            inner_ref[part, (i - 1) * cols : i * cols] = (at(across_ref, i) + along).astype(
+                jnp.bfloat16
+            )
+
+
+def converge(east, north):
     hour_count, row_count, cols = east.shape
-    count = 2 * freqs.shape[1]
     f32, bf16 = jnp.float32, jnp.bfloat16
     return pl.pallas_call(
-        inner_kernel,
+        converge_kernel,
         out_shape=[
-            jax.ShapeDtypeStruct((count, (row_count - 2) * cols), bf16),
-            jax.ShapeDtypeStruct((count, count), f32),
+            jax.ShapeDtypeStruct((hour_count, (row_count - 2) * cols), bf16),
             jax.ShapeDtypeStruct((hour_count, 2 * cols), f32),
             jax.ShapeDtypeStruct((hour_count, cols), bf16),
             jax.ShapeDtypeStruct((hour_count, cols), bf16),
-            jax.ShapeDtypeStruct((hour_count, count), bf16),
-            jax.ShapeDtypeStruct((count, hour_count), bf16),
         ],
-        in_specs=[VMEM, HBM, HBM],
-        out_specs=[VMEM] * 7,
+        in_specs=[HBM, HBM],
+        out_specs=[VMEM] * 4,
         scratch_shapes=[
             pltpu.VMEM(east.shape, east.dtype),
             pltpu.VMEM(north.shape, north.dtype),
@@ -166,17 +152,65 @@
             pltpu.VMEM((hour_count * row_count, cols), f32),
             pltpu.SemaphoreType.DMA((IN_STEPS, 2)),
         ],
-        compiler_params=pltpu.CompilerParams(vmem_limit_bytes=INNER_MIB * MIB),
+        compiler_params=pltpu.CompilerParams(vmem_limit_bytes=CONVERGE_KIB * 1024),
+        name="converge",
+    )(east, north)
+
+
+def inner_kernel(freqs_ref, inner_ref, bands_ref, core_ref, table_ref, waves_ref):
+    hour_count, cells = inner_ref.shape
+    freqs = freqs_ref[...]
+    table = wave_table(jnp.concatenate([freqs, freqs], axis=1), hour_count)
+    waves = table.T.astype(jnp.bfloat16)
+    table_ref[...] = table.astype(jnp.bfloat16)
+    waves_ref[...] = waves
+    core = None
+    for i in range(0, cells, 256):
+        part = slice(i, i + 256)
+        bands = dot(waves, inner_ref[:, part]).astype(jnp.bfloat16)
+        bands_ref[:, part] = bands
+        product = dot_t(bands, bands)
+        core = product if core is None else core + product
+    core_ref[...] = core
+
+
+def inner(freqs, unrounded):
+    hour_count, cells = unrounded.shape
+    count = 2 * freqs.shape[1]
+    f32, bf16 = jnp.float32, jnp.bfloat16
+    flops = 2 * count * cells * (hour_count + count)
+    return pl.pallas_call(
+        inner_kernel,
+        out_shape=[
+            jax.ShapeDtypeStruct((count, cells), bf16),
+            jax.ShapeDtypeStruct((count, count), f32),
+            jax.ShapeDtypeStruct((hour_count, count), bf16),
+            jax.ShapeDtypeStruct((count, hour_count), bf16),
+        ],
+        in_specs=[VMEM] * 2,
+        out_specs=[VMEM] * 4,
+        cost_estimate=pl.CostEstimate(flops=flops, bytes_accessed=6 * MIB, transcendentals=0),
+        compiler_params=pltpu.CompilerParams(vmem_limit_bytes=16 * MIB),
         name="inner",
-    )(freqs, east, north)
+    )(freqs, unrounded)
 
 
 def outer_kernel(
-    tile_count, edge_ref, near_ref, far_ref, waves_ref, core_ref, bands_ref, kept_ref, given_ref
+    tile_count,
+    edge_ref,
+    near_ref,
+    this_ref,
+    that_ref,
+    waves_ref,
+    core_ref,
+    bands_ref,
+    kept_ref,
+    given_ref,
 ):
     cols = near_ref.shape[1]
-    near, far = near_ref[...].astype(jnp.float32), far_ref[...].astype(jnp.float32)
     tile = lax.axis_index("tile")
+    far = jnp.where((tile // 2 + tile) % 2 == 1, this_ref[...], that_ref[...]).astype(jnp.float32)
+    near = near_ref[...].astype(jnp.float32)
     far = jnp.where((tile > 0) & (tile < tile_count - 1), far, 0.0)
     even = tile % 2 == 0
     first = edge_ref[:, :cols] - 0.5 * jnp.where(even, far, near)
@@ -194,17 +228,17 @@
     given_ref[...] = jnp.where(low, packed[half:], packed[:half])
 
 
-def outer(tile_count, edge, near, far, waves, core):
+def outer(tile_count, edge, near, this, that, waves, core):
     count = waves.shape[0]
     half = jax.ShapeDtypeStruct((count // 2, count // 3 * 2), jnp.float32)
     return pl.pallas_call(
         functools.partial(outer_kernel, tile_count),
         out_shape=[jax.ShapeDtypeStruct((count, edge.shape[1]), jnp.bfloat16), half, half],
-        in_specs=[VMEM] * 5,
+        in_specs=[VMEM] * 6,
         out_specs=[VMEM] * 3,
         compiler_params=pltpu.CompilerParams(vmem_limit_bytes=16 * MIB),
         name="outer",
-    )(edge, near, far, waves, core)
+    )(edge, near, this, that, waves, core)
 
 
 def summed(kept, given, axis, beside):
@@ -385,13 +419,14 @@
     tile_count = lax.axis_size("tile")
     cell_total = row_count * col_count * tile_count
     scale = (2.0 / hour_count) ** 2 / cell_total
-    bands, core, edge, near, far, table, waves = inner(band_freqs[None], flux_east, flux_north)
+    converged, edge, near, far = converge(flux_east, flux_north)
+    this = lax.ppermute(far, "tile", across_pairs(tile_count, 0))
+    that = lax.ppermute(far, "tile", across_pairs(tile_count, 1))
     near = lax.ppermute(near, "tile", partners(tile_count, 1))
-    ring = [(i, (i + (1 if i % 2 else -1)) % tile_count) for i in range(tile_count)]
-    far = lax.ppermute(far, "tile", ring)
+    bands, core, table, waves = inner(band_freqs[None], converged)
     start = start_basis.T / jnp.max(jnp.abs(start_basis.T), axis=1, keepdims=True)
     start = exact_dot_t(start, waves.astype(jnp.float32))
-    edge_bands, kept, given = outer(tile_count, edge, near, far, waves, core)
+    edge_bands, kept, given = outer(tile_count, edge, near, this, that, waves, core)
 
     def filtered(part):
         product = jnp.dot(table, part, preferred_element_type=jnp.float32)

time: 40.8 us -> 36.5 us (0.89)
  waiting for transfers between devices: 13.7 us -> 7.73 us
  starting transfers between devices: 8.12 us -> 12 us
  Pallas kernels: 16.2 us -> 14.8 us
  matrix products: 2.31 us -> 0.98 us
    ppermute x3, waiting for transfers between devices: 11.5 us -> 5.31 us  [summed(): kept = kept + lax.ppermute(kept, axis, partners(count, mask + 1))]
    ppermute x3, starting transfers between devices: 1.71 us -> 7.25 us  [summed(): kept = kept + lax.ppermute(kept, axis, partners(count, mask + 1))]
    ppermute x1 -> x2, starting transfers between devices: 5.64 us -> 4.27 us  [the longest x1 3.75 us: body(): this = lax.ppermute(far, 'tile', across_pairs(tile_count, 0))]
    pallas_call x1 -> x2, Pallas kernels: 5.73 us -> 4.39 us  [the longest x1 3.02 us: converge(): pl.pallas_call(converge_kernel, out_shape=[jax.ShapeDtypeStruct((hour_cou...]
    dot_general x2, matrix products: 2.04 us -> 0.71 us  [filtered(): product = jnp.dot(table, part, preferred_element_type=jnp.float32)]
    ppermute x1, starting transfers between devices: 0.52 us -> 0.01 us  [body(): near = lax.ppermute(near, 'tile', partners(tile_count, 1))]
  transfers between devices with their start and end apart: 7 -> 8, of which waited for: 6 -> 6; matrix products, arithmetic and copies ran while one was open for 6% -> 3% of each run, Pallas kernels for 0% -> 4%
where the time goes in v3:
time: 36.5 us; the launch traced here: 36 us
  Pallas kernels  14.8 us (41%)
  starting transfers between devices  12 us (33%)
  waiting for transfers between devices  7.73 us (21%)
  matrix products  0.98 us (3%)
    pallas_call x1, Pallas kernels, project(): pl.pallas_call(functools.partial(project_kernel, scale, lax.axis_size('ti...  9.99 us
    ppermute x3, starting transfers between devices, summed(): kept = kept + lax.ppermute(kept, axis, partners(count, mask + 1))  7.25 us
    ppermute x3, waiting for transfers between devices, summed(): kept = kept + lax.ppermute(kept, axis, partners(count, mask + 1))  5.31 us
    ppermute x1, starting transfers between devices, body(): this = lax.ppermute(far, 'tile', across_pairs(tile_count, 0))  3.75 us
    pallas_call x1, Pallas kernels, converge(): pl.pallas_call(converge_kernel, out_shape=[jax.ShapeDtypeStruct((hour_cou...  3.02 us
    pallas_call x1, Pallas kernels, inner(): pl.pallas_call(inner_kernel, out_shape=[jax.ShapeDtypeStruct((count, cell...  1.37 us
    ppermute x1, waiting for transfers between devices, summed(): kept = kept + lax.ppermute(given, axis, partners(count, 1))  0.92 us
    ppermute x1, waiting for transfers between devices, summed(): return (kept, lax.ppermute(kept, axis, partners(count, 1)), beside)  0.9 us
  transfers between devices with their start and end apart: 8, of which 6 were waited for; matrix products, arithmetic and copies ran while one was open for 3% of the time, Pallas kernels for 4%

profile of v3, /device:TPU:0, one launch (start us, length us, event | category | flops | bytes accessed | tf_op | source)
XLA Modules:
  0.0 36.0 jit_solution(12222968937353870893)
XLA Ops:
  0.0 3.0 %converge.1 = (bf16[256,2816]{1,0:T(8,128)(2,1)S(1)}, f32[256,256]{1,0:T(8,128)S(1)}, bf16[256,128]{1,0:T(8,128)(2,1)S(1)}, bf16[256,128]{1,0:T(8,128)(2,1)S(1)}) custom-call(bf16[256,24,128]{2,1,0:T(8,128)(2,1)} %east_hbm.1, bf16[256,24,128]{2,1,0:T(8,128)(2,1)} %north_hbm.1), custom_call_target="tpu_custom_call" | custom-call | tf_op jit(solution)/shard_map/converge/pallas_call | solution.py:138
  3.0 0.5 %collective-permute-start.2 = (bf16[256,128]{1,0:T(8,128)(2,1)S(1)}, bf16[256,128]{1,0:T(8,128)(2,1)S(1)}, u32[]{:S(2)}, u32[]{:S(2)}) collective-permute-start(bf16[256,128]{1,0:T(8,128)(2,1)S(1)} %get-tuple-element.22), channel_id=1, source_target_pairs={{0,1},{1,0},{2,5},{3,4},{4,3},{5,2},{6,9},{7,8},{8,7},{9,6},{10,13... | collective-permute-start | bytes 196616 | tf_op jit(solution)/shard_map/ppermute | solution.py:424
  3.6 3.8 %collective-permute-start.1 = (bf16[256,128]{1,0:T(8,128)(2,1)S(1)}, bf16[256,128]{1,0:T(8,128)(2,1)S(1)}, u32[]{:S(2)}, u32[]{:S(2)}) collective-permute-start(bf16[256,128]{1,0:T(8,128)(2,1)S(1)} %get-tuple-element.22), channel_id=1, source_target_pairs={{0,3},{1,2},{2,1},{3,0},{4,7},{5,6},{6,5},{7,4},{8,11},{9,10},{10,... | collective-permute-start | bytes 196616 | tf_op jit(solution)/shard_map/ppermute | solution.py:423
  7.3 0.0 collective-permute-start
  7.3 1.4 %inner.1 = (bf16[192,2816]{1,0:T(8,128)(2,1)S(1)}, f32[192,192]{1,0:T(8,128)S(1)}, bf16[256,192]{1,0:T(8,128)(2,1)S(1)}, bf16[192,256]{1,0:T(8,128)(2,1)S(1)}) custom-call(s32[1,96]{1,0:T(1,128)S(1)} %bitcast.6, bf16[256,2816]{1,0:T(8,128)(2,1)S(1)} %get-tuple-element.23.inner_ref), custom_call_target="tpu_custom_call" | custom-call | flops 484442112 | bytes 6291456 | tf_op jit(solution)/shard_map/inner/pallas_call | solution.py:182
  8.7 0.0 copy-start.1
  8.7 0.5 %fusion.inside_ref = bf16[256,2816]{1,0:T(8,128)(2,1)S(1)} fusion(bf16[256,192]{1,0:T(8,128)(2,1)S(1)} %get-tuple-element.28.table_ref, bf16[192,2816]{1,0:T(8,128)(2,1)S(1)} %get-tuple-element.29), kind=kOutput, calls=%fused_computation.1 | convolution fusion | flops 278265856 | bytes 2621440 | tf_op jit(solution)/shard_map/dot_general | solution.py:432
  9.2 0.3 copy-done.1
  9.5 0.1 abs_reduce_fusion
  9.7 0.6 %collective-permute-done.1.this_ref = bf16[256,128]{1,0:T(8,128)(2,1)S(1)} collective-permute-done((bf16[256,128]{1,0:T(8,128)(2,1)S(1)}, bf16[256,128]{1,0:T(8,128)(2,1)S(1)}, u32[]{:S(2)}, u32[]{:S(2)}) %collective-permute-start.1) | collective-permute-done | bytes 65568 | tf_op jit(solution)/shard_map/ppermute | solution.py:423
  10.3 0.5 %outer.1 = (bf16[192,256]{1,0:T(8,128)(2,1)S(1)}, f32[96,128]{1,0:T(8,128)S(1)}, f32[96,128]{1,0:T(8,128)S(1)}) custom-call(f32[256,256]{1,0:T(8,128)S(1)} %get-tuple-element.20.edge_ref, bf16[256,128]{1,0:T(8,128)(2,1)S(1)} %collective-permute-done.near_ref, bf16[256,128]{1,0:T(8,128)(2,1)S(1)} %collective-permute-done.1.this_ref, ...), custom_call_target="tpu_custom_call" | custom-call | tf_op jit(solution)/shard_map/outer/pallas_call | solution.py:234
  10.7 0.1 collective-permute-start.3
  10.8 0.3 fusion.2.start_ref
  11.1 0.9 %collective-permute-done.3 = f32[96,128]{1,0:T(8,128)S(1)} collective-permute-done((f32[96,128]{1,0:T(8,128)S(1)}, f32[96,128]{1,0:T(8,128)S(1)}, u32[]{:S(2)}, u32[]{:S(2)}) %collective-permute-start.3) | collective-permute-done | bytes 49184 | tf_op jit(solution)/shard_map/ppermute | solution.py:246
  12.0 2.2 %collective-permute-start.4 = (f32[96,128]{1,0:T(8,128)S(1)}, f32[96,128]{1,0:T(8,128)S(1)}, u32[]{:S(2)}, u32[]{:S(2)}) collective-permute-start(f32[96,128]{1,0:T(8,128)S(1)} %add.12), channel_id=1, source_target_pairs={{0,3},{1,2},{2,1},{3,0},{4,7},{5,6},{6,5},{7,4},{8,11},{9,10},{10,... | collective-permute-start | bytes 147464 | tf_op jit(solution)/shard_map/ppermute | solution.py:249
  14.2 0.2 fusion.1.edges_ref
  14.4 1.6 %collective-permute-done.4 = f32[96,128]{1,0:T(8,128)S(1)} collective-permute-done((f32[96,128]{1,0:T(8,128)S(1)}, f32[96,128]{1,0:T(8,128)S(1)}, u32[]{:S(2)}, u32[]{:S(2)}) %collective-permute-start.4) | collective-permute-done | bytes 49184 | tf_op jit(solution)/shard_map/ppermute | solution.py:249
  16.1 2.1 %collective-permute-start.5 = (f32[96,128]{1,0:T(8,128)S(1)}, f32[96,128]{1,0:T(8,128)S(1)}, u32[]{:S(2)}, u32[]{:S(2)}) collective-permute-start(f32[96,128]{1,0:T(8,128)S(1)} %add.13), channel_id=1, source_target_pairs={{0,5},{1,4},{2,7},{3,6},{4,1},{5,0},{6,3},{7,2},{8,13},{9,12},{10,... | collective-permute-start | bytes 147464 | tf_op jit(solution)/shard_map/ppermute | solution.py:249
  18.1 1.8 %collective-permute-done.5 = f32[96,128]{1,0:T(8,128)S(1)} collective-permute-done((f32[96,128]{1,0:T(8,128)S(1)}, f32[96,128]{1,0:T(8,128)S(1)}, u32[]{:S(2)}, u32[]{:S(2)}) %collective-permute-start.5) | collective-permute-done | bytes 49184 | tf_op jit(solution)/shard_map/ppermute | solution.py:249
  19.9 3.0 %collective-permute-start.6 = (f32[96,128]{1,0:T(8,128)S(1)}, f32[96,128]{1,0:T(8,128)S(1)}, u32[]{:S(2)}, u32[]{:S(2)}) collective-permute-start(f32[96,128]{1,0:T(8,128)S(1)} %add.14), channel_id=1, source_target_pairs={{0,9},{1,8},{2,11},{3,10},{4,13},{5,12},{6,15},{7,14},{8,1},{9,0},... | collective-permute-start | bytes 147464 | tf_op jit(solution)/shard_map/ppermute | solution.py:249
  22.9 1.9 %collective-permute-done.6 = f32[96,128]{1,0:T(8,128)S(1)} collective-permute-done((f32[96,128]{1,0:T(8,128)S(1)}, f32[96,128]{1,0:T(8,128)S(1)}, u32[]{:S(2)}, u32[]{:S(2)}) %collective-permute-start.6) | collective-permute-done | bytes 49184 | tf_op jit(solution)/shard_map/ppermute | solution.py:249
  24.8 0.3 collective-permute-start.7
  25.1 0.9 %collective-permute-done.7.other_ref = f32[96,128]{1,0:T(8,128)S(1)} collective-permute-done((f32[96,128]{1,0:T(8,128)S(1)}, f32[96,128]{1,0:T(8,128)S(1)}, u32[]{:S(2)}, u32[]{:S(2)}) %collective-permute-start.7) | collective-permute-done | bytes 49184 | tf_op jit(solution)/shard_map/ppermute | solution.py:253
  26.0 10.0 %project.1 = bf16[256,24,128]{2,1,0:T(8,128)(2,1)} custom-call(f32[96,128]{1,0:T(8,128)S(1)} %add.15.kept_ref, f32[96,128]{1,0:T(8,128)S(1)} %collective-permute-done.7.other_ref, f32[64,192]{1,0:T(8,128)S(1)} %fusion.2.start_ref, bf16[256,192]{1,0:T(8,128)(2,1)S(1)} %get-tuple-element.28.table_ref, bf16[192,256]{1,0:T(8,128)(2,1)S(1)} %get-tuple-element.24.waves_ref, ...), custom_call_target="tpu_custom_call" | custom-call | tf_op jit(solution)/shard_map/project/pallas_call | solution.py:402
  (8 shorter events, 0.0 us)
Async XLA Ops:
  0.0 7.3 %copy-start = (s32[96]{0:T(128)S(1)}, s32[96]{0:T(128)}, u32[]{:S(2)}) copy-start(s32[96]{0:T(128)} %param.6) | copy-start | bytes 1156
  3.0 6.6 %collective-permute-start.2 = (bf16[256,128]{1,0:T(8,128)(2,1)S(1)}, bf16[256,128]{1,0:T(8,128)(2,1)S(1)}, u32[]{:S(2)}, u32[]{:S(2)}) collective-permute-start(bf16[256,128]{1,0:T(8,128)(2,1)S(1)} %get-tuple-element.22), channel_id=1, source_target_pairs={{0,1},{1,0},{2,5},{3,4},{4,3},{5,2},{6,9},{7,8},{8,7},{9,6},{10,13... | collective-permute-start | bytes 196616 | tf_op jit(solution)/shard_map/ppermute | solution.py:424
  3.6 6.7 %collective-permute-start.1 = (bf16[256,128]{1,0:T(8,128)(2,1)S(1)}, bf16[256,128]{1,0:T(8,128)(2,1)S(1)}, u32[]{:S(2)}, u32[]{:S(2)}) collective-permute-start(bf16[256,128]{1,0:T(8,128)(2,1)S(1)} %get-tuple-element.22), channel_id=1, source_target_pairs={{0,3},{1,2},{2,1},{3,0},{4,7},{5,6},{6,5},{7,4},{8,11},{9,10},{10,... | collective-permute-start | bytes 196616 | tf_op jit(solution)/shard_map/ppermute | solution.py:423
  7.3 2.3 %collective-permute-start = (bf16[256,128]{1,0:T(8,128)(2,1)S(1)}, bf16[256,128]{1,0:T(8,128)(2,1)S(1)}, u32[]{:S(2)}, u32[]{:S(2)}) collective-permute-start(bf16[256,128]{1,0:T(8,128)(2,1)S(1)} %get-tuple-element.21), channel_id=1, source_target_pairs={{0,1},{1,0},{2,3},{3,2},{4,5},{5,4},{6,7},{7,6},{8,9},{9,8},{10,11... | collective-permute-start | bytes 196616 | tf_op jit(solution)/shard_map/ppermute | solution.py:425
  8.7 0.8 %copy-start.1 = (f32[256,64]{0,1:T(8,128)S(1)}, f32[256,64]{0,1:T(8,128)}, u32[]{:S(2)}) copy-start(f32[256,64]{0,1:T(8,128)} %param.7) | copy-start | bytes 196612
  10.7 1.3 %collective-permute-start.3 = (f32[96,128]{1,0:T(8,128)S(1)}, f32[96,128]{1,0:T(8,128)S(1)}, u32[]{:S(2)}, u32[]{:S(2)}) collective-permute-start(f32[96,128]{1,0:T(8,128)S(1)} %get-tuple-element.27), channel_id=1, source_target_pairs={{0,1},{1,0},{2,3},{3,2},{4,5},{5,4},{6,7},{7,6},{8,9},{9,8},{10,11... | collective-permute-start | bytes 147464 | tf_op jit(solution)/shard_map/ppermute | solution.py:246
  12.0 4.0 %collective-permute-start.4 = (f32[96,128]{1,0:T(8,128)S(1)}, f32[96,128]{1,0:T(8,128)S(1)}, u32[]{:S(2)}, u32[]{:S(2)}) collective-permute-start(f32[96,128]{1,0:T(8,128)S(1)} %add.12), channel_id=1, source_target_pairs={{0,3},{1,2},{2,1},{3,0},{4,7},{5,6},{6,5},{7,4},{8,11},{9,10},{10,... | collective-permute-start | bytes 147464 | tf_op jit(solution)/shard_map/ppermute | solution.py:249
  16.1 3.9 %collective-permute-start.5 = (f32[96,128]{1,0:T(8,128)S(1)}, f32[96,128]{1,0:T(8,128)S(1)}, u32[]{:S(2)}, u32[]{:S(2)}) collective-permute-start(f32[96,128]{1,0:T(8,128)S(1)} %add.13), channel_id=1, source_target_pairs={{0,5},{1,4},{2,7},{3,6},{4,1},{5,0},{6,3},{7,2},{8,13},{9,12},{10,... | collective-permute-start | bytes 147464 | tf_op jit(solution)/shard_map/ppermute | solution.py:249
  19.9 4.8 %collective-permute-start.6 = (f32[96,128]{1,0:T(8,128)S(1)}, f32[96,128]{1,0:T(8,128)S(1)}, u32[]{:S(2)}, u32[]{:S(2)}) collective-permute-start(f32[96,128]{1,0:T(8,128)S(1)} %add.14), channel_id=1, source_target_pairs={{0,9},{1,8},{2,11},{3,10},{4,13},{5,12},{6,15},{7,14},{8,1},{9,0},... | collective-permute-start | bytes 147464 | tf_op jit(solution)/shard_map/ppermute | solution.py:249
  24.8 1.2 %collective-permute-start.7 = (f32[96,128]{1,0:T(8,128)S(1)}, f32[96,128]{1,0:T(8,128)S(1)}, u32[]{:S(2)}, u32[]{:S(2)}) collective-permute-start(f32[96,128]{1,0:T(8,128)S(1)} %add.15.kept_ref), channel_id=1, source_target_pairs={{0,1},{1,0},{2,3},{3,2},{4,5},{5,4},{6,7},{7,6},{8,9},{9,8},{10,11... | collective-permute-start | bytes 147464 | tf_op jit(solution)/shard_map/ppermute | solution.py:253

commit v4 on v3

--- a/solution.py
+++ b/solution.py
@@ -9,11 +9,11 @@
 from jax.sharding import PartitionSpec as P
 
 ITERS = 4
-WIDE = 16
+WIDE = 8
 IN_STEPS = 4
 OUT_STEPS = 4
+EARLY = 4
 CONVERGE_KIB = 52736
-EXACT = lax.Precision.HIGHEST
 VMEM = pl.BlockSpec(memory_space=pltpu.VMEM)
 HBM = pl.BlockSpec(memory_space=pltpu.HBM)
 MIB = 2**20
@@ -63,16 +63,29 @@
     return lax.dot_general(a, b, (((1,), (1,)), ((), ())), preferred_element_type=jnp.float32)
 
 
+def thirds(x):
+    high = x.astype(jnp.bfloat16)
+    rest = x - high.astype(jnp.float32)
+    middle = rest.astype(jnp.bfloat16)
+    return high, middle, (rest - middle.astype(jnp.float32)).astype(jnp.bfloat16)
+
+
+def by_thirds(a, b, product):
+    n = a.shape[0]
+    high, middle, low = thirds(a)
+    by_high, by_middle, by_low = thirds(b)
+    two = jnp.concatenate([high, middle], axis=0)
+    p = product(jnp.concatenate([two, low], axis=0), by_high)
+    q, r = product(two, by_middle), product(high, by_low)
+    return p[:n] + ((p[n : 2 * n] + q[:n]) + (p[2 * n :] + q[n:] + r))
+
+
 def exact_dot(a, b):
-    return lax.dot_general(
-        a, b, (((1,), (0,)), ((), ())), precision=EXACT, preferred_element_type=jnp.float32
-    )
+    return by_thirds(a, b, dot)
 
 
 def exact_dot_t(a, b):
-    return lax.dot_general(
-        a, b, (((1,), (1,)), ((), ())), precision=EXACT, preferred_element_type=jnp.float32
-    )
+    return by_thirds(a, b, dot_t)
 
 
 def cross_band(cols):
@@ -254,11 +267,11 @@
 
 
 def lane(v, j):
-    return jnp.broadcast_to(v[:, j : j + 1], v.shape)
+    return jnp.take_along_axis(v, jnp.full(v.shape, j, jnp.int32), axis=1)
 
 
 def row(v, k):
-    return jnp.broadcast_to(v[k : k + 1, :], v.shape)
+    return jnp.take_along_axis(v, jnp.full(v.shape, k, jnp.int32), axis=0)
 
 
 def assembled(rows, place):
@@ -278,47 +291,60 @@
     joined = jnp.concatenate([crossed, eye], axis=1)
     strips = [joined[s : s + 8] for s in range(0, size, 8)]
     place = lax.broadcasted_iota(jnp.int32, strips[0].shape, 0)
-    out = []
+    rows, early = [], []
     for start in range(0, size, WIDE):
-        first, last = start // 8, min(size, start + 2 * WIDE) // 8
-        cols = [[lane(s, start + k) for s in strips[first:last]] for k in range(WIDE)]
-        rows = []
+        first = start // 8
+        cols = early + [
+            [lane(s, start + k) for s in strips[first:]] for k in range(len(early), WIDE)
+        ]
+        ahead = range(start + WIDE, min(size, start + WIDE + EARLY))
+        early = [[lane(s, j) for s in strips[first:]] for j in ahead]
         for k in range(0, WIDE, 2):
             q, s = k // 8, k % 8
             a, b, c = row(cols[k][q], s), row(cols[k][q], s + 1), row(cols[k + 1][q], s + 1)
-            det = a * c - b * b
-            inv = pl.reciprocal(det, approx=True)
+            inv_a = pl.reciprocal(a, approx=True)
+            m = b * inv_a
+            pivot = c - b * m
+            inv_c = pl.reciprocal(pivot, approx=True)
             below = place > s + 1
             u = [jnp.where(below, cols[k][q], 0.0)] + cols[k][q + 1 :]
             v = [jnp.where(below, cols[k + 1][q], 0.0)] + cols[k + 1][q + 1 :]
-            x = [i * c - j * b for i, j in zip(u, v)]
-            y = [j * a - i * b for i, j in zip(u, v)]
+            v = [j - i * m for i, j in zip(u, v)]
 
             def eliminate(target, offset):
                 top, low = row(target[offset], s), row(target[offset], s + 1)
-                top_inv, low_inv = top * inv, low * inv
-                for i in range(len(x)):
-                    target[offset + i] = (target[offset + i] - x[i] * top_inv) - y[i] * low_inv
+                low = low - top * m
+                x, y = top * inv_a, low * inv_c
+                for i in range(len(u)):
+                    target[offset + i] = (target[offset + i] - u[i] * x) - v[i] * y
                 return top, low
 
-            for later in cols[k + 2 :]:
+            for later in cols[k + 2 :] + early:
                 eliminate(later, q)
             top, low = eliminate(strips, first + q)
-            ra = lax.rsqrt(a)
-            rows += [top * ra, (a * low - b * top) * (ra * lax.rsqrt(det))]
-        out.append(assembled(rows, place))
-        if 8 * last < size:
-            update = exact_dot(out[-1].T[8 * last : size], out[-1])
-            for i in range(last, size // 8):
-                strips[i] = strips[i] - update[8 * (i - last) : 8 * (i - last) + 8]
-    return jnp.concatenate(out, axis=0)[:, size:]
-
-
-def thirds(x):
-    high = x.astype(jnp.bfloat16)
-    rest = x - high.astype(jnp.float32)
-    middle = rest.astype(jnp.bfloat16)
-    return high, middle, (rest - middle.astype(jnp.float32)).astype(jnp.bfloat16)
+            rows += [top * lax.rsqrt(a), low * lax.rsqrt(pivot)]
+        early = [col[WIDE // 8 :] for col in early]
+    return assembled(rows, place)
+
+
+def stacked(a, b):
+    size = a.shape[1] // 2
+    left = lax.broadcasted_iota(jnp.int32, a.shape, 1) < size
+    high, middle, low = thirds(jnp.where(left, pltpu.roll(a, size, 1), a))
+    two = jnp.where(left, high, middle)
+    by_high, by_middle, by_low = thirds(b)
+    return [
+        (
+            jnp.concatenate([two, jnp.where(left, high, low)], axis=1),
+            jnp.concatenate([by_high, by_high, by_middle, by_high], axis=0),
+        ),
+        (two, jnp.concatenate([by_low, by_middle], axis=0)),
+    ]
+
+
+def inverse_dot(inverse, b):
+    (a, x), (c, y) = stacked(inverse, b)
+    return dot(a, x) + dot(c, y)
 
 
 def project_kernel(
@@ -352,9 +378,6 @@
         ],
         axis=0,
     )
-    ids = [lax.broadcasted_iota(jnp.int32, (size, size), d) for d in range(2)]
-    trace = jnp.sum(jnp.where(ids[0] == ids[1], b00 + b11 + b22, 0.0), keepdims=True)
-    unit = 1.0 / (trace * (hour_count / 2))
     waves = waves_ref[...]
 
     def by_waves(x):
@@ -362,17 +385,16 @@
         return high + (middle + rest)
 
     panel = by_waves(exact_dot(start_ref[...], core))
-    crossed = exact_dot_t(panel, panel) * unit * unit
-    panel = panel * unit
+    crossed = exact_dot_t(panel, panel)
     table = table_ref[...]
     high, middle, rest = (dot(table, part) for part in thirds(by_waves(core)))
-    gram = (high + (middle + rest)) * unit
+    gram = high + (middle + rest)
     for sweep in range(ITERS):
         inverse = inverse_factor(crossed)
         if sweep < ITERS - 1:
-            panel = exact_dot(inverse, exact_dot(panel, gram))
+            panel = inverse_dot(inverse, exact_dot(panel, gram))
             crossed = exact_dot_t(panel, panel)
-    basis_t = exact_dot(inverse, panel)
+    basis_t = inverse_dot(inverse, panel)
     basis = basis_t.T.astype(jnp.bfloat16)
     basis_t = basis_t.astype(jnp.bfloat16)
     parts = [(inside_ref[:, i * cols : (i + 2) * cols], i + 1, i + 2) for i in range(0, row_count - 2, 2)]
@@ -424,8 +446,7 @@
     that = lax.ppermute(far, "tile", across_pairs(tile_count, 1))
     near = lax.ppermute(near, "tile", partners(tile_count, 1))
     bands, core, table, waves = inner(band_freqs[None], converged)
-    start = start_basis.T / jnp.max(jnp.abs(start_basis.T), axis=1, keepdims=True)
-    start = exact_dot_t(start, waves.astype(jnp.float32))
+    start = jnp.dot(start_basis.T, waves.T.astype(jnp.float32), precision=lax.Precision.HIGHEST)
     edge_bands, kept, given = outer(tile_count, edge, near, this, that, waves, core)
 
     def filtered(part):

time: 36.5 us -> 35.5 us (0.973)
  Pallas kernels: 14.8 us -> 13.9 us
  waiting for transfers between devices: 7.73 us -> 8.17 us
    pallas_call x1, Pallas kernels: 9.99 us -> 8.98 us  [project(): pl.pallas_call(functools.partial(project_kernel, scale, lax.axis_size('ti...]
    ppermute x1, waiting for transfers between devices: 0.59 us -> 1.01 us  [body(): this = lax.ppermute(far, 'tile', across_pairs(tile_count, 0))]
where the time goes in v4:
time: 35.5 us; the launch traced here: 35.1 us
  Pallas kernels  13.9 us (39%)
  starting transfers between devices  12 us (34%)
  waiting for transfers between devices  8.17 us (23%)
  matrix products  0.94 us (3%)
    pallas_call x1, Pallas kernels, project(): pl.pallas_call(functools.partial(project_kernel, scale, lax.axis_size('ti...  8.98 us
    ppermute x3, starting transfers between devices, summed(): kept = kept + lax.ppermute(kept, axis, partners(count, mask + 1))  7.26 us
    ppermute x3, waiting for transfers between devices, summed(): kept = kept + lax.ppermute(kept, axis, partners(count, mask + 1))  5.31 us
    ppermute x1, starting transfers between devices, body(): this = lax.ppermute(far, 'tile', across_pairs(tile_count, 0))  3.75 us
    pallas_call x1, Pallas kernels, converge(): pl.pallas_call(converge_kernel, out_shape=[jax.ShapeDtypeStruct((hour_cou...  3.05 us
    pallas_call x1, Pallas kernels, inner(): pl.pallas_call(inner_kernel, out_shape=[jax.ShapeDtypeStruct((count, cell...  1.37 us
    ppermute x1, waiting for transfers between devices, body(): this = lax.ppermute(far, 'tile', across_pairs(tile_count, 0))  1.01 us
    ppermute x1, waiting for transfers between devices, summed(): kept = kept + lax.ppermute(given, axis, partners(count, 1))  0.95 us
  transfers between devices with their start and end apart: 8, of which 6 were waited for; matrix products, arithmetic and copies ran while one was open for 3% of the time, Pallas kernels for 4%

profile of v4, /device:TPU:0, one launch (start us, length us, event | category | flops | bytes accessed | tf_op | source)
XLA Modules:
  0.0 35.1 jit_solution(6479308882814207177)
XLA Ops:
  0.0 0.0 copy-start
  0.0 3.1 %converge.1 = (bf16[256,2816]{1,0:T(8,128)(2,1)S(1)}, f32[256,256]{1,0:T(8,128)S(1)}, bf16[256,128]{1,0:T(8,128)(2,1)S(1)}, bf16[256,128]{1,0:T(8,128)(2,1)S(1)}) custom-call(bf16[256,24,128]{2,1,0:T(8,128)(2,1)} %east_hbm.1, bf16[256,24,128]{2,1,0:T(8,128)(2,1)} %north_hbm.1), custom_call_target="tpu_custom_call" | custom-call | tf_op jit(solution)/shard_map/converge/pallas_call | solution.py:151
  3.1 0.5 %collective-permute-start.2 = (bf16[256,128]{1,0:T(8,128)(2,1)S(1)}, bf16[256,128]{1,0:T(8,128)(2,1)S(1)}, u32[]{:S(2)}, u32[]{:S(2)}) collective-permute-start(bf16[256,128]{1,0:T(8,128)(2,1)S(1)} %get-tuple-element.22), channel_id=1, source_target_pairs={{0,1},{1,0},{2,5},{3,4},{4,3},{5,2},{6,9},{7,8},{8,7},{9,6},{10,13... | collective-permute-start | bytes 196616 | tf_op jit(solution)/shard_map/ppermute | solution.py:446
  3.6 3.8 %collective-permute-start.1 = (bf16[256,128]{1,0:T(8,128)(2,1)S(1)}, bf16[256,128]{1,0:T(8,128)(2,1)S(1)}, u32[]{:S(2)}, u32[]{:S(2)}) collective-permute-start(bf16[256,128]{1,0:T(8,128)(2,1)S(1)} %get-tuple-element.22), channel_id=1, source_target_pairs={{0,3},{1,2},{2,1},{3,0},{4,7},{5,6},{6,5},{7,4},{8,11},{9,10},{10,... | collective-permute-start | bytes 196616 | tf_op jit(solution)/shard_map/ppermute | solution.py:445
  7.3 0.0 collective-permute-start
  7.3 1.4 %inner.1 = (bf16[192,2816]{1,0:T(8,128)(2,1)S(1)}, f32[192,192]{1,0:T(8,128)S(1)}, bf16[256,192]{1,0:T(8,128)(2,1)S(1)}, bf16[192,256]{1,0:T(8,128)(2,1)S(1)}) custom-call(s32[1,96]{1,0:T(1,128)S(1)} %bitcast.9, bf16[256,2816]{1,0:T(8,128)(2,1)S(1)} %get-tuple-element.23.inner_ref), custom_call_target="tpu_custom_call" | custom-call | flops 484442112 | bytes 6291456 | tf_op jit(solution)/shard_map/inner/pallas_call | solution.py:195
  8.7 0.5 %fusion.inside_ref = bf16[256,2816]{1,0:T(8,128)(2,1)S(1)} fusion(bf16[256,192]{1,0:T(8,128)(2,1)S(1)} %get-tuple-element.28.table_ref, bf16[192,2816]{1,0:T(8,128)(2,1)S(1)} %get-tuple-element.29), kind=kOutput, calls=%fused_computation.1 | convolution fusion | flops 278265856 | bytes 2621440 | tf_op jit(solution)/shard_map/dot_general | solution.py:453
  9.3 0.0 collective-permute-done.near_ref
  9.3 0.0 collective-permute-done.2.that_ref
  9.3 1.0 %collective-permute-done.1.this_ref = bf16[256,128]{1,0:T(8,128)(2,1)S(1)} collective-permute-done((bf16[256,128]{1,0:T(8,128)(2,1)S(1)}, bf16[256,128]{1,0:T(8,128)(2,1)S(1)}, u32[]{:S(2)}, u32[]{:S(2)}) %collective-permute-start.1) | collective-permute-done | bytes 65568 | tf_op jit(solution)/shard_map/ppermute | solution.py:445
  10.3 0.5 %outer.1 = (bf16[192,256]{1,0:T(8,128)(2,1)S(1)}, f32[96,128]{1,0:T(8,128)S(1)}, f32[96,128]{1,0:T(8,128)S(1)}) custom-call(f32[256,256]{1,0:T(8,128)S(1)} %get-tuple-element.20.edge_ref, bf16[256,128]{1,0:T(8,128)(2,1)S(1)} %collective-permute-done.near_ref, bf16[256,128]{1,0:T(8,128)(2,1)S(1)} %collective-permute-done.1.this_ref, ...), custom_call_target="tpu_custom_call" | custom-call | tf_op jit(solution)/shard_map/outer/pallas_call | solution.py:247
  10.8 0.1 collective-permute-start.3
  10.9 0.2 convolution_bitcast_fusion.start_ref
  11.1 0.9 %collective-permute-done.3 = f32[96,128]{1,0:T(8,128)S(1)} collective-permute-done((f32[96,128]{1,0:T(8,128)S(1)}, f32[96,128]{1,0:T(8,128)S(1)}, u32[]{:S(2)}, u32[]{:S(2)}) %collective-permute-start.3) | collective-permute-done | bytes 49184 | tf_op jit(solution)/shard_map/ppermute | solution.py:259
  12.1 2.2 %collective-permute-start.4 = (f32[96,128]{1,0:T(8,128)S(1)}, f32[96,128]{1,0:T(8,128)S(1)}, u32[]{:S(2)}, u32[]{:S(2)}) collective-permute-start(f32[96,128]{1,0:T(8,128)S(1)} %add.12), channel_id=1, source_target_pairs={{0,3},{1,2},{2,1},{3,0},{4,7},{5,6},{6,5},{7,4},{8,11},{9,10},{10,... | collective-permute-start | bytes 147464 | tf_op jit(solution)/shard_map/ppermute | solution.py:262
  14.3 0.2 fusion.1.edges_ref
  14.4 1.6 %collective-permute-done.4 = f32[96,128]{1,0:T(8,128)S(1)} collective-permute-done((f32[96,128]{1,0:T(8,128)S(1)}, f32[96,128]{1,0:T(8,128)S(1)}, u32[]{:S(2)}, u32[]{:S(2)}) %collective-permute-start.4) | collective-permute-done | bytes 49184 | tf_op jit(solution)/shard_map/ppermute | solution.py:262
  16.1 2.1 %collective-permute-start.5 = (f32[96,128]{1,0:T(8,128)S(1)}, f32[96,128]{1,0:T(8,128)S(1)}, u32[]{:S(2)}, u32[]{:S(2)}) collective-permute-start(f32[96,128]{1,0:T(8,128)S(1)} %add.13), channel_id=1, source_target_pairs={{0,5},{1,4},{2,7},{3,6},{4,1},{5,0},{6,3},{7,2},{8,13},{9,12},{10,... | collective-permute-start | bytes 147464 | tf_op jit(solution)/shard_map/ppermute | solution.py:262
  18.2 1.8 %collective-permute-done.5 = f32[96,128]{1,0:T(8,128)S(1)} collective-permute-done((f32[96,128]{1,0:T(8,128)S(1)}, f32[96,128]{1,0:T(8,128)S(1)}, u32[]{:S(2)}, u32[]{:S(2)}) %collective-permute-start.5) | collective-permute-done | bytes 49184 | tf_op jit(solution)/shard_map/ppermute | solution.py:262
  20.0 3.0 %collective-permute-start.6 = (f32[96,128]{1,0:T(8,128)S(1)}, f32[96,128]{1,0:T(8,128)S(1)}, u32[]{:S(2)}, u32[]{:S(2)}) collective-permute-start(f32[96,128]{1,0:T(8,128)S(1)} %add.14), channel_id=1, source_target_pairs={{0,9},{1,8},{2,11},{3,10},{4,13},{5,12},{6,15},{7,14},{8,1},{9,0},... | collective-permute-start | bytes 147464 | tf_op jit(solution)/shard_map/ppermute | solution.py:262
  23.0 1.9 %collective-permute-done.6 = f32[96,128]{1,0:T(8,128)S(1)} collective-permute-done((f32[96,128]{1,0:T(8,128)S(1)}, f32[96,128]{1,0:T(8,128)S(1)}, u32[]{:S(2)}, u32[]{:S(2)}) %collective-permute-start.6) | collective-permute-done | bytes 49184 | tf_op jit(solution)/shard_map/ppermute | solution.py:262
  24.8 0.3 collective-permute-start.7
  25.2 0.9 %collective-permute-done.7.other_ref = f32[96,128]{1,0:T(8,128)S(1)} collective-permute-done((f32[96,128]{1,0:T(8,128)S(1)}, f32[96,128]{1,0:T(8,128)S(1)}, u32[]{:S(2)}, u32[]{:S(2)}) %collective-permute-start.7) | collective-permute-done | bytes 49184 | tf_op jit(solution)/shard_map/ppermute | solution.py:266
  26.1 9.0 %project.1 = bf16[256,24,128]{2,1,0:T(8,128)(2,1)} custom-call(f32[96,128]{1,0:T(8,128)S(1)} %add.15.kept_ref, f32[96,128]{1,0:T(8,128)S(1)} %collective-permute-done.7.other_ref, f32[64,192]{1,0:T(8,128)S(1)} %convolution_bitcast_fusion.start_ref, bf16[256,192]{1,0:T(8,128)(2,1)S(1)} %get-tuple-element.28.table_ref, ...), custom_call_target="tpu_custom_call" | custom-call | tf_op jit(solution)/shard_map/project/pallas_call | solution.py:424
  (7 shorter events, 0.0 us)
Async XLA Ops:
  0.0 10.9 %copy-start = (f32[256,64]{0,1:T(8,128)S(1)}, f32[256,64]{0,1:T(8,128)}, u32[]{:S(2)}) copy-start(f32[256,64]{0,1:T(8,128)} %param.7) | copy-start | bytes 196612
  0.0 7.3 %copy-start.1 = (s32[96]{0:T(128)S(1)}, s32[96]{0:T(128)}, u32[]{:S(2)}) copy-start(s32[96]{0:T(128)} %param.6) | copy-start | bytes 1156
  3.1 6.2 %collective-permute-start.2 = (bf16[256,128]{1,0:T(8,128)(2,1)S(1)}, bf16[256,128]{1,0:T(8,128)(2,1)S(1)}, u32[]{:S(2)}, u32[]{:S(2)}) collective-permute-start(bf16[256,128]{1,0:T(8,128)(2,1)S(1)} %get-tuple-element.22), channel_id=1, source_target_pairs={{0,1},{1,0},{2,5},{3,4},{4,3},{5,2},{6,9},{7,8},{8,7},{9,6},{10,13... | collective-permute-start | bytes 196616 | tf_op jit(solution)/shard_map/ppermute | solution.py:446
  3.6 6.7 %collective-permute-start.1 = (bf16[256,128]{1,0:T(8,128)(2,1)S(1)}, bf16[256,128]{1,0:T(8,128)(2,1)S(1)}, u32[]{:S(2)}, u32[]{:S(2)}) collective-permute-start(bf16[256,128]{1,0:T(8,128)(2,1)S(1)} %get-tuple-element.22), channel_id=1, source_target_pairs={{0,3},{1,2},{2,1},{3,0},{4,7},{5,6},{6,5},{7,4},{8,11},{9,10},{10,... | collective-permute-start | bytes 196616 | tf_op jit(solution)/shard_map/ppermute | solution.py:445
  7.3 1.9 %collective-permute-start = (bf16[256,128]{1,0:T(8,128)(2,1)S(1)}, bf16[256,128]{1,0:T(8,128)(2,1)S(1)}, u32[]{:S(2)}, u32[]{:S(2)}) collective-permute-start(bf16[256,128]{1,0:T(8,128)(2,1)S(1)} %get-tuple-element.21), channel_id=1, source_target_pairs={{0,1},{1,0},{2,3},{3,2},{4,5},{5,4},{6,7},{7,6},{8,9},{9,8},{10,11... | collective-permute-start | bytes 196616 | tf_op jit(solution)/shard_map/ppermute | solution.py:447
  10.8 1.3 %collective-permute-start.3 = (f32[96,128]{1,0:T(8,128)S(1)}, f32[96,128]{1,0:T(8,128)S(1)}, u32[]{:S(2)}, u32[]{:S(2)}) collective-permute-start(f32[96,128]{1,0:T(8,128)S(1)} %get-tuple-element.27), channel_id=1, source_target_pairs={{0,1},{1,0},{2,3},{3,2},{4,5},{5,4},{6,7},{7,6},{8,9},{9,8},{10,11... | collective-permute-start | bytes 147464 | tf_op jit(solution)/shard_map/ppermute | solution.py:259
  12.1 4.0 %collective-permute-start.4 = (f32[96,128]{1,0:T(8,128)S(1)}, f32[96,128]{1,0:T(8,128)S(1)}, u32[]{:S(2)}, u32[]{:S(2)}) collective-permute-start(f32[96,128]{1,0:T(8,128)S(1)} %add.12), channel_id=1, source_target_pairs={{0,3},{1,2},{2,1},{3,0},{4,7},{5,6},{6,5},{7,4},{8,11},{9,10},{10,... | collective-permute-start | bytes 147464 | tf_op jit(solution)/shard_map/ppermute | solution.py:262
  16.1 3.9 %collective-permute-start.5 = (f32[96,128]{1,0:T(8,128)S(1)}, f32[96,128]{1,0:T(8,128)S(1)}, u32[]{:S(2)}, u32[]{:S(2)}) collective-permute-start(f32[96,128]{1,0:T(8,128)S(1)} %add.13), channel_id=1, source_target_pairs={{0,5},{1,4},{2,7},{3,6},{4,1},{5,0},{6,3},{7,2},{8,13},{9,12},{10,... | collective-permute-start | bytes 147464 | tf_op jit(solution)/shard_map/ppermute | solution.py:262
  20.0 4.8 %collective-permute-start.6 = (f32[96,128]{1,0:T(8,128)S(1)}, f32[96,128]{1,0:T(8,128)S(1)}, u32[]{:S(2)}, u32[]{:S(2)}) collective-permute-start(f32[96,128]{1,0:T(8,128)S(1)} %add.14), channel_id=1, source_target_pairs={{0,9},{1,8},{2,11},{3,10},{4,13},{5,12},{6,15},{7,14},{8,1},{9,0},... | collective-permute-start | bytes 147464 | tf_op jit(solution)/shard_map/ppermute | solution.py:262
  24.8 1.2 %collective-permute-start.7 = (f32[96,128]{1,0:T(8,128)S(1)}, f32[96,128]{1,0:T(8,128)S(1)}, u32[]{:S(2)}, u32[]{:S(2)}) collective-permute-start(f32[96,128]{1,0:T(8,128)S(1)} %add.15.kept_ref), channel_id=1, source_target_pairs={{0,1},{1,0},{2,3},{3,2},{4,5},{5,4},{6,7},{7,6},{8,9},{9,8},{10,11... | collective-permute-start | bytes 147464 | tf_op jit(solution)/shard_map/ppermute | solution.py:266

commit v5 on v4

--- a/solution.py
+++ b/solution.py
@@ -208,6 +208,41 @@
     )(freqs, unrounded)
 
 
+def square_ids(size):
+    return [lax.broadcasted_iota(jnp.int32, (size, size), d) for d in range(2)]
+
+
+def pack(core):
+    size = core.shape[0] // 3
+    b00, b10, b20 = (core[i * size : (i + 1) * size, :size] for i in range(3))
+    b11, b21 = (core[i * size : (i + 1) * size, size : 2 * size] for i in (1, 2))
+    i, j = square_ids(size)
+    diagonal = jnp.sum(jnp.where(i == j, b11, 0.0), axis=0, keepdims=True)
+    shared = jnp.where(i >= j, b00, b11)
+    third = jnp.where((i == 0) & (j > 0), diagonal, core[2 * size :, 2 * size :])
+    third = jnp.where((i == 1) & (j == size - 1), diagonal[:, :1], third)
+    half = size // 2
+    pairs = ((b10, b20), (b21[:half], b21[half:]), (shared, third))
+    return jnp.concatenate([jnp.concatenate(pair, axis=1) for pair in pairs], axis=0)
+
+
+def unpack(packed):
+    size = packed.shape[1] // 2
+    half = size // 2
+    top, middle, bottom = packed[:size], packed[size : size + half], packed[size + half :]
+    b10, b20 = top[:, :size], top[:, size:]
+    b21 = jnp.concatenate([middle[:, :size], middle[:, size:]], axis=0)
+    shared, third = bottom[:, :size], bottom[:, size:]
+    i, j = square_ids(size)
+    turned = shared.T
+    diagonal = jnp.where(j == 0, third[1:2, size - 1 :], third[:1])
+    b00 = jnp.where(i >= j, shared, turned)
+    b11 = jnp.where(i < j, shared, jnp.where(i > j, turned, diagonal))
+    b22 = jnp.where(i >= j, third, third.T)
+    rows = ((b00, b10.T, b20.T), (b10, b11, b21.T), (b20, b21, b22))
+    return jnp.concatenate([jnp.concatenate(row, axis=1) for row in rows], axis=0)
+
+
 def outer_kernel(
     tile_count,
     edge_ref,
@@ -232,9 +267,7 @@
     bands = dot(waves_ref[...], jnp.concatenate(pair, axis=1)).astype(jnp.bfloat16)
     bands_ref[...] = bands
     core = core_ref[...] + dot_t(bands, bands)
-    size = core.shape[0] // 3
-    right = jnp.concatenate([core[size:, size : 2 * size], core[2 * size :, 2 * size :]], axis=0)
-    packed = jnp.concatenate([core[:, :size], right], axis=1)
+    packed = pack(core)
     half = packed.shape[0] // 2
     low = parity(tile, tile_count) == 0
     kept_ref[...] = jnp.where(low, packed[:half], packed[half:])
@@ -243,7 +276,7 @@
 
 def outer(tile_count, edge, near, this, that, waves, core):
     count = waves.shape[0]
-    half = jax.ShapeDtypeStruct((count // 2, count // 3 * 2), jnp.float32)
+    half = jax.ShapeDtypeStruct((count // 12 * 5, count // 3 * 2), jnp.float32)
     return pl.pallas_call(
         functools.partial(outer_kernel, tile_count),
         out_shape=[jax.ShapeDtypeStruct((count, edge.shape[1]), jnp.bfloat16), half, half],
@@ -366,18 +399,7 @@
     kept, other = kept_ref[...], other_ref[...]
     low = parity(lax.axis_index("tile"), tile_count) == 0
     blocks = jnp.concatenate([jnp.where(low, kept, other), jnp.where(low, other, kept)], axis=0)
-    blocks = blocks * scale
-    size = blocks.shape[1] // 2
-    b00, b10, b20 = (blocks[i * size : (i + 1) * size, :size] for i in range(3))
-    b11, b21, b22 = (blocks[i * size : (i + 1) * size, size:] for i in range(3))
-    core = jnp.concatenate(
-        [
-            jnp.concatenate([b00, b10.T, b20.T], axis=1),
-            jnp.concatenate([b10, b11, b21.T], axis=1),
-            jnp.concatenate([b20, b21, b22], axis=1),
-        ],
-        axis=0,
-    )
+    core = unpack(blocks * scale)
     waves = waves_ref[...]
 
     def by_waves(x):

time: 35.5 us -> 34.6 us (0.975)
  waiting for transfers between devices: 8.17 us -> 7.69 us
  starting transfers between devices: 12 us -> 11.6 us
    ppermute x3, waiting for transfers between devices: 5.31 us -> 4.87 us  [summed(): kept = kept + lax.ppermute(kept, axis, partners(count, mask + 1))]
where the time goes in v5:
time: 34.6 us; the launch traced here: 34.4 us
  Pallas kernels  14.1 us (41%)
  starting transfers between devices  11.6 us (34%)
  waiting for transfers between devices  7.69 us (22%)
  matrix products  0.94 us (3%)
    pallas_call x1, Pallas kernels, project(): pl.pallas_call(functools.partial(project_kernel, scale, lax.axis_size('ti...  9.05 us
    ppermute x3, starting transfers between devices, summed(): kept = kept + lax.ppermute(kept, axis, partners(count, mask + 1))  6.96 us
    ppermute x3, waiting for transfers between devices, summed(): kept = kept + lax.ppermute(kept, axis, partners(count, mask + 1))  4.87 us
    ppermute x1, starting transfers between devices, body(): this = lax.ppermute(far, 'tile', across_pairs(tile_count, 0))  3.75 us
    pallas_call x1, Pallas kernels, converge(): pl.pallas_call(converge_kernel, out_shape=[jax.ShapeDtypeStruct((hour_cou...  3.05 us
    pallas_call x1, Pallas kernels, inner(): pl.pallas_call(inner_kernel, out_shape=[jax.ShapeDtypeStruct((count, cell...  1.37 us
    ppermute x1, waiting for transfers between devices, body(): this = lax.ppermute(far, 'tile', across_pairs(tile_count, 0))  1.01 us
    ppermute x1, waiting for transfers between devices, summed(): kept = kept + lax.ppermute(given, axis, partners(count, 1))  0.94 us
  transfers between devices with their start and end apart: 8, of which 6 were waited for; matrix products, arithmetic and copies ran while one was open for 3% of the time, Pallas kernels for 4%

profile of v5, /device:TPU:0, one launch (start us, length us, event | category | flops | bytes accessed | tf_op | source)
XLA Modules:
  0.0 34.4 jit_solution(13410123853504751282)
XLA Ops:
  0.0 0.0 copy-start
  0.0 3.1 %converge.1 = (bf16[256,2816]{1,0:T(8,128)(2,1)S(1)}, f32[256,256]{1,0:T(8,128)S(1)}, bf16[256,128]{1,0:T(8,128)(2,1)S(1)}, bf16[256,128]{1,0:T(8,128)(2,1)S(1)}) custom-call(bf16[256,24,128]{2,1,0:T(8,128)(2,1)} %east_hbm.1, bf16[256,24,128]{2,1,0:T(8,128)(2,1)} %north_hbm.1), custom_call_target="tpu_custom_call" | custom-call | tf_op jit(solution)/shard_map/converge/pallas_call | solution.py:151
  3.1 0.5 %collective-permute-start.2 = (bf16[256,128]{1,0:T(8,128)(2,1)S(1)}, bf16[256,128]{1,0:T(8,128)(2,1)S(1)}, u32[]{:S(2)}, u32[]{:S(2)}) collective-permute-start(bf16[256,128]{1,0:T(8,128)(2,1)S(1)} %get-tuple-element.22), channel_id=1, source_target_pairs={{0,1},{1,0},{2,5},{3,4},{4,3},{5,2},{6,9},{7,8},{8,7},{9,6},{10,13... | collective-permute-start | bytes 196616 | tf_op jit(solution)/shard_map/ppermute | solution.py:468
  3.6 3.8 %collective-permute-start.1 = (bf16[256,128]{1,0:T(8,128)(2,1)S(1)}, bf16[256,128]{1,0:T(8,128)(2,1)S(1)}, u32[]{:S(2)}, u32[]{:S(2)}) collective-permute-start(bf16[256,128]{1,0:T(8,128)(2,1)S(1)} %get-tuple-element.22), channel_id=1, source_target_pairs={{0,3},{1,2},{2,1},{3,0},{4,7},{5,6},{6,5},{7,4},{8,11},{9,10},{10,... | collective-permute-start | bytes 196616 | tf_op jit(solution)/shard_map/ppermute | solution.py:467
  7.3 0.0 collective-permute-start
  7.3 1.4 %inner.1 = (bf16[192,2816]{1,0:T(8,128)(2,1)S(1)}, f32[192,192]{1,0:T(8,128)S(1)}, bf16[256,192]{1,0:T(8,128)(2,1)S(1)}, bf16[192,256]{1,0:T(8,128)(2,1)S(1)}) custom-call(s32[1,96]{1,0:T(1,128)S(1)} %bitcast.9, bf16[256,2816]{1,0:T(8,128)(2,1)S(1)} %get-tuple-element.23.inner_ref), custom_call_target="tpu_custom_call" | custom-call | flops 484442112 | bytes 6291456 | tf_op jit(solution)/shard_map/inner/pallas_call | solution.py:195
  8.7 0.5 %fusion.inside_ref = bf16[256,2816]{1,0:T(8,128)(2,1)S(1)} fusion(bf16[256,192]{1,0:T(8,128)(2,1)S(1)} %get-tuple-element.28.table_ref, bf16[192,2816]{1,0:T(8,128)(2,1)S(1)} %get-tuple-element.29), kind=kOutput, calls=%fused_computation.1 | convolution fusion | flops 278265856 | bytes 2621440 | tf_op jit(solution)/shard_map/dot_general | solution.py:475
  9.3 0.0 collective-permute-done.near_ref
  9.3 0.0 collective-permute-done.2.that_ref
  9.3 1.0 %collective-permute-done.1.this_ref = bf16[256,128]{1,0:T(8,128)(2,1)S(1)} collective-permute-done((bf16[256,128]{1,0:T(8,128)(2,1)S(1)}, bf16[256,128]{1,0:T(8,128)(2,1)S(1)}, u32[]{:S(2)}, u32[]{:S(2)}) %collective-permute-start.1) | collective-permute-done | bytes 65568 | tf_op jit(solution)/shard_map/ppermute | solution.py:467
  10.3 0.6 %outer.1 = (bf16[192,256]{1,0:T(8,128)(2,1)S(1)}, f32[80,128]{1,0:T(8,128)S(1)}, f32[80,128]{1,0:T(8,128)S(1)}) custom-call(f32[256,256]{1,0:T(8,128)S(1)} %get-tuple-element.20.edge_ref, bf16[256,128]{1,0:T(8,128)(2,1)S(1)} %collective-permute-done.near_ref, bf16[256,128]{1,0:T(8,128)(2,1)S(1)} %collective-permute-done.1.this_ref, ...), custom_call_target="tpu_custom_call" | custom-call | tf_op jit(solution)/shard_map/outer/pallas_call | solution.py:280
  10.9 0.1 collective-permute-start.3
  10.9 0.2 convolution_bitcast_fusion.start_ref
  11.2 0.9 %collective-permute-done.3 = f32[80,128]{1,0:T(8,128)S(1)} collective-permute-done((f32[80,128]{1,0:T(8,128)S(1)}, f32[80,128]{1,0:T(8,128)S(1)}, u32[]{:S(2)}, u32[]{:S(2)}) %collective-permute-start.3) | collective-permute-done | bytes 40992 | tf_op jit(solution)/shard_map/ppermute | solution.py:292
  12.1 2.2 %collective-permute-start.4 = (f32[80,128]{1,0:T(8,128)S(1)}, f32[80,128]{1,0:T(8,128)S(1)}, u32[]{:S(2)}, u32[]{:S(2)}) collective-permute-start(f32[80,128]{1,0:T(8,128)S(1)} %add.12), channel_id=1, source_target_pairs={{0,3},{1,2},{2,1},{3,0},{4,7},{5,6},{6,5},{7,4},{8,11},{9,10},{10,... | collective-permute-start | bytes 122888 | tf_op jit(solution)/shard_map/ppermute | solution.py:295
  14.3 0.2 fusion.1.edges_ref
  14.5 1.5 %collective-permute-done.4 = f32[80,128]{1,0:T(8,128)S(1)} collective-permute-done((f32[80,128]{1,0:T(8,128)S(1)}, f32[80,128]{1,0:T(8,128)S(1)}, u32[]{:S(2)}, u32[]{:S(2)}) %collective-permute-start.4) | collective-permute-done | bytes 40992 | tf_op jit(solution)/shard_map/ppermute | solution.py:295
  16.0 1.9 %collective-permute-start.5 = (f32[80,128]{1,0:T(8,128)S(1)}, f32[80,128]{1,0:T(8,128)S(1)}, u32[]{:S(2)}, u32[]{:S(2)}) collective-permute-start(f32[80,128]{1,0:T(8,128)S(1)} %add.13), channel_id=1, source_target_pairs={{0,5},{1,4},{2,7},{3,6},{4,1},{5,0},{6,3},{7,2},{8,13},{9,12},{10,... | collective-permute-start | bytes 122888 | tf_op jit(solution)/shard_map/ppermute | solution.py:295
  17.9 1.7 %collective-permute-done.5 = f32[80,128]{1,0:T(8,128)S(1)} collective-permute-done((f32[80,128]{1,0:T(8,128)S(1)}, f32[80,128]{1,0:T(8,128)S(1)}, u32[]{:S(2)}, u32[]{:S(2)}) %collective-permute-start.5) | collective-permute-done | bytes 40992 | tf_op jit(solution)/shard_map/ppermute | solution.py:295
  19.6 2.9 %collective-permute-start.6 = (f32[80,128]{1,0:T(8,128)S(1)}, f32[80,128]{1,0:T(8,128)S(1)}, u32[]{:S(2)}, u32[]{:S(2)}) collective-permute-start(f32[80,128]{1,0:T(8,128)S(1)} %add.14), channel_id=1, source_target_pairs={{0,9},{1,8},{2,11},{3,10},{4,13},{5,12},{6,15},{7,14},{8,1},{9,0},... | collective-permute-start | bytes 122888 | tf_op jit(solution)/shard_map/ppermute | solution.py:295
  22.5 1.7 %collective-permute-done.6 = f32[80,128]{1,0:T(8,128)S(1)} collective-permute-done((f32[80,128]{1,0:T(8,128)S(1)}, f32[80,128]{1,0:T(8,128)S(1)}, u32[]{:S(2)}, u32[]{:S(2)}) %collective-permute-start.6) | collective-permute-done | bytes 40992 | tf_op jit(solution)/shard_map/ppermute | solution.py:295
  24.2 0.3 %collective-permute-start.7 = (f32[80,128]{1,0:T(8,128)S(1)}, f32[80,128]{1,0:T(8,128)S(1)}, u32[]{:S(2)}, u32[]{:S(2)}) collective-permute-start(f32[80,128]{1,0:T(8,128)S(1)} %add.15.kept_ref), channel_id=1, source_target_pairs={{0,1},{1,0},{2,3},{3,2},{4,5},{5,4},{6,7},{7,6},{8,9},{9,8},{10,11... | collective-permute-start | bytes 122888 | tf_op jit(solution)/shard_map/ppermute | solution.py:299
  24.5 0.9 %collective-permute-done.7.other_ref = f32[80,128]{1,0:T(8,128)S(1)} collective-permute-done((f32[80,128]{1,0:T(8,128)S(1)}, f32[80,128]{1,0:T(8,128)S(1)}, u32[]{:S(2)}, u32[]{:S(2)}) %collective-permute-start.7) | collective-permute-done | bytes 40992 | tf_op jit(solution)/shard_map/ppermute | solution.py:299
  25.4 9.1 %project.1 = bf16[256,24,128]{2,1,0:T(8,128)(2,1)} custom-call(f32[80,128]{1,0:T(8,128)S(1)} %add.15.kept_ref, f32[80,128]{1,0:T(8,128)S(1)} %collective-permute-done.7.other_ref, f32[64,192]{1,0:T(8,128)S(1)} %convolution_bitcast_fusion.start_ref, bf16[256,192]{1,0:T(8,128)(2,1)S(1)} %get-tuple-element.28.table_ref, ...), custom_call_target="tpu_custom_call" | custom-call | tf_op jit(solution)/shard_map/project/pallas_call | solution.py:446
  (7 shorter events, 0.0 us)
Async XLA Ops:
  0.0 10.9 %copy-start = (f32[256,64]{0,1:T(8,128)S(1)}, f32[256,64]{0,1:T(8,128)}, u32[]{:S(2)}) copy-start(f32[256,64]{0,1:T(8,128)} %param.7) | copy-start | bytes 196612
  0.0 7.3 %copy-start.1 = (s32[96]{0:T(128)S(1)}, s32[96]{0:T(128)}, u32[]{:S(2)}) copy-start(s32[96]{0:T(128)} %param.6) | copy-start | bytes 1156
  3.1 6.2 %collective-permute-start.2 = (bf16[256,128]{1,0:T(8,128)(2,1)S(1)}, bf16[256,128]{1,0:T(8,128)(2,1)S(1)}, u32[]{:S(2)}, u32[]{:S(2)}) collective-permute-start(bf16[256,128]{1,0:T(8,128)(2,1)S(1)} %get-tuple-element.22), channel_id=1, source_target_pairs={{0,1},{1,0},{2,5},{3,4},{4,3},{5,2},{6,9},{7,8},{8,7},{9,6},{10,13... | collective-permute-start | bytes 196616 | tf_op jit(solution)/shard_map/ppermute | solution.py:468
  3.6 6.7 %collective-permute-start.1 = (bf16[256,128]{1,0:T(8,128)(2,1)S(1)}, bf16[256,128]{1,0:T(8,128)(2,1)S(1)}, u32[]{:S(2)}, u32[]{:S(2)}) collective-permute-start(bf16[256,128]{1,0:T(8,128)(2,1)S(1)} %get-tuple-element.22), channel_id=1, source_target_pairs={{0,3},{1,2},{2,1},{3,0},{4,7},{5,6},{6,5},{7,4},{8,11},{9,10},{10,... | collective-permute-start | bytes 196616 | tf_op jit(solution)/shard_map/ppermute | solution.py:467
  7.3 1.9 %collective-permute-start = (bf16[256,128]{1,0:T(8,128)(2,1)S(1)}, bf16[256,128]{1,0:T(8,128)(2,1)S(1)}, u32[]{:S(2)}, u32[]{:S(2)}) collective-permute-start(bf16[256,128]{1,0:T(8,128)(2,1)S(1)} %get-tuple-element.21), channel_id=1, source_target_pairs={{0,1},{1,0},{2,3},{3,2},{4,5},{5,4},{6,7},{7,6},{8,9},{9,8},{10,11... | collective-permute-start | bytes 196616 | tf_op jit(solution)/shard_map/ppermute | solution.py:469
  10.9 1.2 %collective-permute-start.3 = (f32[80,128]{1,0:T(8,128)S(1)}, f32[80,128]{1,0:T(8,128)S(1)}, u32[]{:S(2)}, u32[]{:S(2)}) collective-permute-start(f32[80,128]{1,0:T(8,128)S(1)} %get-tuple-element.27), channel_id=1, source_target_pairs={{0,1},{1,0},{2,3},{3,2},{4,5},{5,4},{6,7},{7,6},{8,9},{9,8},{10,11... | collective-permute-start | bytes 122888 | tf_op jit(solution)/shard_map/ppermute | solution.py:292
  12.1 3.9 %collective-permute-start.4 = (f32[80,128]{1,0:T(8,128)S(1)}, f32[80,128]{1,0:T(8,128)S(1)}, u32[]{:S(2)}, u32[]{:S(2)}) collective-permute-start(f32[80,128]{1,0:T(8,128)S(1)} %add.12), channel_id=1, source_target_pairs={{0,3},{1,2},{2,1},{3,0},{4,7},{5,6},{6,5},{7,4},{8,11},{9,10},{10,... | collective-permute-start | bytes 122888 | tf_op jit(solution)/shard_map/ppermute | solution.py:295
  16.0 3.6 %collective-permute-start.5 = (f32[80,128]{1,0:T(8,128)S(1)}, f32[80,128]{1,0:T(8,128)S(1)}, u32[]{:S(2)}, u32[]{:S(2)}) collective-permute-start(f32[80,128]{1,0:T(8,128)S(1)} %add.13), channel_id=1, source_target_pairs={{0,5},{1,4},{2,7},{3,6},{4,1},{5,0},{6,3},{7,2},{8,13},{9,12},{10,... | collective-permute-start | bytes 122888 | tf_op jit(solution)/shard_map/ppermute | solution.py:295
  19.6 4.5 %collective-permute-start.6 = (f32[80,128]{1,0:T(8,128)S(1)}, f32[80,128]{1,0:T(8,128)S(1)}, u32[]{:S(2)}, u32[]{:S(2)}) collective-permute-start(f32[80,128]{1,0:T(8,128)S(1)} %add.14), channel_id=1, source_target_pairs={{0,9},{1,8},{2,11},{3,10},{4,13},{5,12},{6,15},{7,14},{8,1},{9,0},... | collective-permute-start | bytes 122888 | tf_op jit(solution)/shard_map/ppermute | solution.py:295
  24.2 1.2 %collective-permute-start.7 = (f32[80,128]{1,0:T(8,128)S(1)}, f32[80,128]{1,0:T(8,128)S(1)}, u32[]{:S(2)}, u32[]{:S(2)}) collective-permute-start(f32[80,128]{1,0:T(8,128)S(1)} %add.15.kept_ref), channel_id=1, source_target_pairs={{0,1},{1,0},{2,3},{3,2},{4,5},{5,4},{6,7},{7,6},{8,9},{9,8},{10,11... | collective-permute-start | bytes 122888 | tf_op jit(solution)/shard_map/ppermute | solution.py:299

commit v6 on v5

--- a/solution.py
+++ b/solution.py
@@ -94,48 +94,56 @@
     return band.astype(jnp.bfloat16)
 
 
-def converge_kernel(
+def inner_kernel(
+    freqs_ref,
     east_hbm,
     north_hbm,
-    inner_ref,
+    bands_ref,
+    core_ref,
     edge_ref,
-    near_ref,
-    far_ref,
+    table_ref,
+    waves_ref,
     east_ref,
     north_ref,
     along_ref,
     across_ref,
+    inner_ref,
     sems,
 ):
     hour_count, row_count, cols = east_ref.shape
     steps = sems.shape[0]
     hours = hour_count // steps
     flat = hours * row_count
-    arrays = ((east_hbm, east_ref), (north_hbm, north_ref))
-    parts = [slice(step * hours, (step + 1) * hours) for step in range(steps)]
-    copies = [
-        [pltpu.make_async_copy(a.at[p], b.at[p], sems.at[i, k]) for k, (a, b) in enumerate(arrays)]
-        for i, p in enumerate(parts)
-    ]
-    for pair in copies:
-        for copy in pair:
+
+    def copies(step):
+        part = slice(step * hours, (step + 1) * hours)
+        return [
+            pltpu.make_async_copy(src.at[part], dst.at[part], sems.at[step, k])
+            for k, (src, dst) in enumerate(((east_hbm, east_ref), (north_hbm, north_ref)))
+        ]
+
+    for step in range(steps):
+        for copy in copies(step):
             copy.start()
+    freqs = freqs_ref[...]
+    table = wave_table(jnp.concatenate([freqs, freqs], axis=1), hour_count)
+    waves = table.T.astype(jnp.bfloat16)
+    table_ref[...] = table.astype(jnp.bfloat16)
+    waves_ref[...] = waves
     band = cross_band(cols)
-    for step, part in enumerate(parts):
-        for copy in copies[step]:
+    for step in range(steps):
+        for copy in copies(step):
             copy.wait()
+        part = slice(step * hours, (step + 1) * hours)
         to = slice(step * flat, (step + 1) * flat)
         along_ref[to] = 0.5 * east_ref[part].astype(jnp.float32).reshape(flat, cols)
         north = north_ref[part].astype(jnp.float32).reshape(flat, cols).astype(jnp.bfloat16)
         across_ref[to] = dot(north, band)
 
+
         def at(ref, i):
             return ref[pl.ds(step * flat + i, hours, stride=row_count)]
 
-        head, tail = at(along_ref, 0) * 2.0, at(along_ref, row_count - 1) * 2.0
-        even = lax.axis_index("tile") % 2 == 0
-        near_ref[part] = jnp.where(even, tail, head).astype(jnp.bfloat16)
-        far_ref[part] = jnp.where(even, head, tail).astype(jnp.bfloat16)
         edge_ref[part, :cols] = at(across_ref, 0) + at(along_ref, 1)
         edge_ref[part, cols:] = at(across_ref, row_count - 1) - at(along_ref, row_count - 2)
         for i in range(1, row_count - 1):
@@ -143,69 +151,42 @@
             inner_ref[part, (i - 1) * cols : i * cols] = (at(across_ref, i) + along).astype(
                 jnp.bfloat16
             )
-
-
-def converge(east, north):
+    core = None
+    for i in range(0, row_count - 2, 2):
+        pair = slice(i * cols, (i + 2) * cols)
+        bands = dot(waves, inner_ref[:, pair]).astype(jnp.bfloat16)
+        bands_ref[:, pair] = bands
+        product = dot_t(bands, bands)
+        core = product if core is None else core + product
+    core_ref[...] = core
+
+
+def inner(freqs, east, north):
     hour_count, row_count, cols = east.shape
+    count = 2 * freqs.shape[1]
     f32, bf16 = jnp.float32, jnp.bfloat16
     return pl.pallas_call(
-        converge_kernel,
+        inner_kernel,
         out_shape=[
-            jax.ShapeDtypeStruct((hour_count, (row_count - 2) * cols), bf16),
+            jax.ShapeDtypeStruct((count, (row_count - 2) * cols), bf16),
+            jax.ShapeDtypeStruct((count, count), f32),
             jax.ShapeDtypeStruct((hour_count, 2 * cols), f32),
-            jax.ShapeDtypeStruct((hour_count, cols), bf16),
-            jax.ShapeDtypeStruct((hour_count, cols), bf16),
+            jax.ShapeDtypeStruct((hour_count, count), bf16),
+            jax.ShapeDtypeStruct((count, hour_count), bf16),
         ],
-        in_specs=[HBM, HBM],
-        out_specs=[VMEM] * 4,
+        in_specs=[VMEM, HBM, HBM],
+        out_specs=[VMEM] * 5,
         scratch_shapes=[
             pltpu.VMEM(east.shape, east.dtype),
             pltpu.VMEM(north.shape, north.dtype),
             pltpu.VMEM((hour_count * row_count, cols), f32),
             pltpu.VMEM((hour_count * row_count, cols), f32),
+            pltpu.VMEM((hour_count, (row_count - 2) * cols), bf16),
             pltpu.SemaphoreType.DMA((IN_STEPS, 2)),
         ],
         compiler_params=pltpu.CompilerParams(vmem_limit_bytes=CONVERGE_KIB * 1024),
-        name="converge",
-    )(east, north)
-
-
-def inner_kernel(freqs_ref, inner_ref, bands_ref, core_ref, table_ref, waves_ref):
-    hour_count, cells = inner_ref.shape
-    freqs = freqs_ref[...]
-    table = wave_table(jnp.concatenate([freqs, freqs], axis=1), hour_count)
-    waves = table.T.astype(jnp.bfloat16)
-    table_ref[...] = table.astype(jnp.bfloat16)
-    waves_ref[...] = waves
-    core = None
-    for i in range(0, cells, 256):
-        part = slice(i, i + 256)
-        bands = dot(waves, inner_ref[:, part]).astype(jnp.bfloat16)
-        bands_ref[:, part] = bands
-        product = dot_t(bands, bands)
-        core = product if core is None else core + product
-    core_ref[...] = core
-
-
-def inner(freqs, unrounded):
-    hour_count, cells = unrounded.shape
-    count = 2 * freqs.shape[1]
-    f32, bf16 = jnp.float32, jnp.bfloat16
-    flops = 2 * count * cells * (hour_count + count)
-    return pl.pallas_call(
-        inner_kernel,
-        out_shape=[
-            jax.ShapeDtypeStruct((count, cells), bf16),
-            jax.ShapeDtypeStruct((count, count), f32),
-            jax.ShapeDtypeStruct((hour_count, count), bf16),
-            jax.ShapeDtypeStruct((count, hour_count), bf16),
-        ],
-        in_specs=[VMEM] * 2,
-        out_specs=[VMEM] * 4,
-        cost_estimate=pl.CostEstimate(flops=flops, bytes_accessed=6 * MIB, transcendentals=0),
-        compiler_params=pltpu.CompilerParams(vmem_limit_bytes=16 * MIB),
         name="inner",
-    )(freqs, unrounded)
+    )(freqs, east, north)
 
 
 def square_ids(size):
@@ -463,13 +444,16 @@
     tile_count = lax.axis_size("tile")
     cell_total = row_count * col_count * tile_count
     scale = (2.0 / hour_count) ** 2 / cell_total
-    converged, edge, near, far = converge(flux_east, flux_north)
+    even = lax.axis_index("tile") % 2 == 0
+    head, tail = flux_east[:, 0], flux_east[:, -1]
+    near, far = jnp.where(even, tail, head), jnp.where(even, head, tail)
     this = lax.ppermute(far, "tile", across_pairs(tile_count, 0))
     that = lax.ppermute(far, "tile", across_pairs(tile_count, 1))
     near = lax.ppermute(near, "tile", partners(tile_count, 1))
-    bands, core, table, waves = inner(band_freqs[None], converged)
+    bands, core, edge, table, waves = inner(band_freqs[None], flux_east, flux_north)
     start = jnp.dot(start_basis.T, waves.T.astype(jnp.float32), precision=lax.Precision.HIGHEST)
     edge_bands, kept, given = outer(tile_count, edge, near, this, that, waves, core)
+    bands, given = lax.optimization_barrier((bands, given))
 
     def filtered(part):
         product = jnp.dot(table, part, preferred_element_type=jnp.float32)

time: 34.6 us -> 34.2 us (0.988)
  starting transfers between devices: 11.6 us -> 9.37 us
  local copies, waits for them, and re-layouts: 0.01 us -> 2.1 us
  Pallas kernels: 14.1 us -> 13.5 us
    ppermute x3, starting transfers between devices: 6.96 us -> 4.22 us  [summed(): kept = kept + lax.ppermute(kept, axis, partners(count, mask + 1))]
    ppermute x3, waiting for transfers between devices: 4.87 us -> 6.78 us  [summed(): kept = kept + lax.ppermute(kept, axis, partners(count, mask + 1))]
    slice x0 -> x1, local copies, waits for them, and re-layouts: none -> 1.44 us  [body(): head, tail = (flux_east[:, 0], flux_east[:, -1])]
    ppermute x1, waiting for transfers between devices: 1.01 us -> 0.01 us  [body(): this = lax.ppermute(far, 'tile', across_pairs(tile_count, 0))]
    unnamed x4, local copies, waits for them, and re-layouts: 0.01 us -> 0.66 us
    ppermute x1, waiting for transfers between devices: 0.94 us -> 0.34 us  [summed(): kept = kept + lax.ppermute(given, axis, partners(count, 1))]
    pallas_call x2 -> x1, Pallas kernels: 4.43 us -> 3.84 us  [inner(): pl.pallas_call(inner_kernel, out_shape=[jax.ShapeDtypeStruct((count, (row...]
    ppermute x1, starting transfers between devices: 0.05 us -> 0.53 us  [summed(): kept = kept + lax.ppermute(given, axis, partners(count, 1))]
  transfers between devices with their start and end apart: 8 -> 8, of which waited for: 6 -> 5; matrix products, arithmetic and copies ran while one was open for 3% -> 3% of each run, Pallas kernels for 4% -> 11%
where the time goes in v6:
time: 34.2 us; the launch traced here: 34 us
  Pallas kernels  13.5 us (39%)
  starting transfers between devices  9.37 us (27%)
  waiting for transfers between devices  7.99 us (23%)
  local copies, waits for them, and re-layouts  2.1 us (6%)
  matrix products  0.95 us (3%)
    pallas_call x1, Pallas kernels, project(): pl.pallas_call(functools.partial(project_kernel, scale, lax.axis_size('ti...  9.05 us
    ppermute x3, waiting for transfers between devices, summed(): kept = kept + lax.ppermute(kept, axis, partners(count, mask + 1))  6.78 us
    ppermute x3, starting transfers between devices, summed(): kept = kept + lax.ppermute(kept, axis, partners(count, mask + 1))  4.22 us
    pallas_call x1, Pallas kernels, inner(): pl.pallas_call(inner_kernel, out_shape=[jax.ShapeDtypeStruct((count, (row...  3.84 us
    ppermute x1, starting transfers between devices, body(): this = lax.ppermute(far, 'tile', across_pairs(tile_count, 0))  3.75 us
    slice x1, local copies, waits for them, and re-layouts, body(): head, tail = (flux_east[:, 0], flux_east[:, -1])  1.44 us
    ppermute x1, waiting for transfers between devices, summed(): return (kept, lax.ppermute(kept, axis, partners(count, 1)), beside)  0.87 us
    dot_general x2, matrix products, filtered(): product = jnp.dot(table, part, preferred_element_type=jnp.float32)  0.71 us
  transfers between devices with their start and end apart: 8, of which 5 were waited for; matrix products, arithmetic and copies ran while one was open for 3% of the time, Pallas kernels for 11%

profile of v6, /device:TPU:0, one launch (start us, length us, event | category | flops | bytes accessed | tf_op | source)
XLA Modules:
  0.0 34.0 jit_solution(9287184095363560501)
XLA Ops:
  0.0 1.4 %fusion.2 = (bf16[256,1,128]{2,1,0:T(2,128)(2,1)S(1)}, bf16[256,1,128]{2,1,0:T(2,128)(2,1)S(1)}) fusion(bf16[256,24,128]{2,1,0:T(8,128)(2,1)} %east_hbm.1), kind=kLoop, calls=%fused_computation.7 | loop fusion | bytes 262144 | tf_op jit(solution)/shard_map/slice | solution.py:448
  1.5 0.5 %collective-permute-start.2 = (bf16[256,128]{1,0:T(8,128)(2,1)S(1)}, bf16[256,128]{1,0:T(8,128)(2,1)S(1)}, u32[]{:S(2)}, u32[]{:S(2)}) collective-permute-start(bf16[256,128]{1,0:T(8,128)(2,1)S(1)} %get-tuple-element.35), channel_id=1, source_target_pairs={{0,1},{1,0},{2,5},{3,4},{4,3},{5,2},{6,9},{7,8},{8,7},{9,6},{10,13... | collective-permute-start | bytes 196616 | tf_op jit(solution)/shard_map/ppermute | solution.py:451
  2.0 3.8 %collective-permute-start.1 = (bf16[256,128]{1,0:T(8,128)(2,1)S(1)}, bf16[256,128]{1,0:T(8,128)(2,1)S(1)}, u32[]{:S(2)}, u32[]{:S(2)}) collective-permute-start(bf16[256,128]{1,0:T(8,128)(2,1)S(1)} %get-tuple-element.35), channel_id=1, source_target_pairs={{0,3},{1,2},{2,1},{3,0},{4,7},{5,6},{6,5},{7,4},{8,11},{9,10},{10,... | collective-permute-start | bytes 196616 | tf_op jit(solution)/shard_map/ppermute | solution.py:450
  5.7 0.0 collective-permute-start
  5.8 0.7 %copy-done.1 = s32[96]{0:T(128)S(1)} copy-done((s32[96]{0:T(128)S(1)}, s32[96]{0:T(128)}, u32[]{:S(2)}) %copy-start.1) | copy-done | bytes 408
  6.4 3.8 %inner.1 = (bf16[192,2816]{1,0:T(8,128)(2,1)S(1)}, f32[192,192]{1,0:T(8,128)S(1)}, f32[256,256]{1,0:T(8,128)S(1)}, bf16[256,192]{1,0:T(8,128)(2,1)S(1)}, bf16[192,256]{1,0:T(8,128)(2,1)S(1)}) custom-call(s32[1,96]{1,0:T(1,128)S(1)} %bitcast.13, bf16[256,24,128]{2,1,0:T(8,128)(2,1)} %east_hbm.1, bf16[256,24,128]{2,1,0:T(8,128)(2,1)} %north_hbm.1), custom_call_target="tpu_custom_call" | custom-call | tf_op jit(solution)/shard_map/inner/pallas_call | solution.py:168
  10.3 0.2 convolution_bitcast_fusion.start_ref
  10.5 0.0 collective-permute-done.near_ref
  10.5 0.0 collective-permute-done.2.that_ref
  10.5 0.0 collective-permute-done.1.this_ref
  10.5 0.6 %outer.1 = (bf16[192,256]{1,0:T(8,128)(2,1)S(1)}, f32[80,128]{1,0:T(8,128)S(1)}, f32[80,128]{1,0:T(8,128)S(1)}) custom-call(f32[256,256]{1,0:T(8,128)S(1)} %get-tuple-element.19.edge_ref, bf16[256,128]{1,0:T(8,128)(2,1)S(1)} %collective-permute-done.near_ref, bf16[256,128]{1,0:T(8,128)(2,1)S(1)} %collective-permute-done.1.this_ref, ...), custom_call_target="tpu_custom_call" | custom-call | tf_op jit(solution)/shard_map/outer/pallas_call | solution.py:261
  11.1 0.5 %collective-permute-start.3 = (f32[80,128]{1,0:T(8,128)S(1)}, f32[80,128]{1,0:T(8,128)S(1)}, u32[]{:S(2)}, u32[]{:S(2)}) collective-permute-start(f32[80,128]{1,0:T(8,128)S(1)} %get-tuple-element.25), channel_id=1, source_target_pairs={{0,1},{1,0},{2,3},{3,2},{4,5},{5,4},{6,7},{7,6},{8,9},{9,8},{10,11... | collective-permute-start | bytes 122888 | tf_op jit(solution)/shard_map/ppermute | solution.py:273
  11.7 0.5 %fusion.inside_ref = bf16[256,2816]{1,0:T(8,128)(2,1)S(1)} fusion(bf16[256,192]{1,0:T(8,128)(2,1)S(1)} %get-tuple-element.26.table_ref, bf16[192,2816]{1,0:T(8,128)(2,1)S(1)} %get-tuple-element.27), kind=kOutput, calls=%fused_computation.1 | convolution fusion | flops 278265856 | bytes 2621440 | tf_op jit(solution)/shard_map/dot_general | solution.py:459
  12.2 0.3 collective-permute-done.3
  12.5 0.1 collective-permute-start.4
  12.7 0.2 fusion.1.edges_ref
  12.9 3.1 %collective-permute-done.4 = f32[80,128]{1,0:T(8,128)S(1)} collective-permute-done((f32[80,128]{1,0:T(8,128)S(1)}, f32[80,128]{1,0:T(8,128)S(1)}, u32[]{:S(2)}, u32[]{:S(2)}) %collective-permute-start.4) | collective-permute-done | bytes 40992 | tf_op jit(solution)/shard_map/ppermute | solution.py:276
  16.0 1.5 %collective-permute-start.5 = (f32[80,128]{1,0:T(8,128)S(1)}, f32[80,128]{1,0:T(8,128)S(1)}, u32[]{:S(2)}, u32[]{:S(2)}) collective-permute-start(f32[80,128]{1,0:T(8,128)S(1)} %add.18), channel_id=1, source_target_pairs={{0,5},{1,4},{2,7},{3,6},{4,1},{5,0},{6,3},{7,2},{8,13},{9,12},{10,... | collective-permute-start | bytes 122888 | tf_op jit(solution)/shard_map/ppermute | solution.py:276
  17.5 1.9 %collective-permute-done.5 = f32[80,128]{1,0:T(8,128)S(1)} collective-permute-done((f32[80,128]{1,0:T(8,128)S(1)}, f32[80,128]{1,0:T(8,128)S(1)}, u32[]{:S(2)}, u32[]{:S(2)}) %collective-permute-start.5) | collective-permute-done | bytes 40992 | tf_op jit(solution)/shard_map/ppermute | solution.py:276
  19.4 2.5 %collective-permute-start.6 = (f32[80,128]{1,0:T(8,128)S(1)}, f32[80,128]{1,0:T(8,128)S(1)}, u32[]{:S(2)}, u32[]{:S(2)}) collective-permute-start(f32[80,128]{1,0:T(8,128)S(1)} %add.19), channel_id=1, source_target_pairs={{0,9},{1,8},{2,11},{3,10},{4,13},{5,12},{6,15},{7,14},{8,1},{9,0},... | collective-permute-start | bytes 122888 | tf_op jit(solution)/shard_map/ppermute | solution.py:276
  22.0 1.8 %collective-permute-done.6 = f32[80,128]{1,0:T(8,128)S(1)} collective-permute-done((f32[80,128]{1,0:T(8,128)S(1)}, f32[80,128]{1,0:T(8,128)S(1)}, u32[]{:S(2)}, u32[]{:S(2)}) %collective-permute-start.6) | collective-permute-done | bytes 40992 | tf_op jit(solution)/shard_map/ppermute | solution.py:276
  23.7 0.3 %collective-permute-start.7 = (f32[80,128]{1,0:T(8,128)S(1)}, f32[80,128]{1,0:T(8,128)S(1)}, u32[]{:S(2)}, u32[]{:S(2)}) collective-permute-start(f32[80,128]{1,0:T(8,128)S(1)} %add.20.kept_ref), channel_id=1, source_target_pairs={{0,1},{1,0},{2,3},{3,2},{4,5},{5,4},{6,7},{7,6},{8,9},{9,8},{10,11... | collective-permute-start | bytes 122888 | tf_op jit(solution)/shard_map/ppermute | solution.py:280
  24.1 0.9 %collective-permute-done.7.other_ref = f32[80,128]{1,0:T(8,128)S(1)} collective-permute-done((f32[80,128]{1,0:T(8,128)S(1)}, f32[80,128]{1,0:T(8,128)S(1)}, u32[]{:S(2)}, u32[]{:S(2)}) %collective-permute-start.7) | collective-permute-done | bytes 40992 | tf_op jit(solution)/shard_map/ppermute | solution.py:280
  25.0 9.1 %project.1 = bf16[256,24,128]{2,1,0:T(8,128)(2,1)} custom-call(f32[80,128]{1,0:T(8,128)S(1)} %add.20.kept_ref, f32[80,128]{1,0:T(8,128)S(1)} %collective-permute-done.7.other_ref, f32[64,192]{1,0:T(8,128)S(1)} %convolution_bitcast_fusion.start_ref, bf16[256,192]{1,0:T(8,128)(2,1)S(1)} %get-tuple-element.26.table_ref, ...), custom_call_target="tpu_custom_call" | custom-call | tf_op jit(solution)/shard_map/project/pallas_call | solution.py:427
  (8 shorter events, 0.1 us)
Async XLA Ops:
  0.0 10.3 %copy-start = (f32[256,64]{0,1:T(8,128)S(1)}, f32[256,64]{0,1:T(8,128)}, u32[]{:S(2)}) copy-start(f32[256,64]{0,1:T(8,128)} %param.7) | copy-start | bytes 196612
  1.5 9.1 %collective-permute-start.2 = (bf16[256,128]{1,0:T(8,128)(2,1)S(1)}, bf16[256,128]{1,0:T(8,128)(2,1)S(1)}, u32[]{:S(2)}, u32[]{:S(2)}) collective-permute-start(bf16[256,128]{1,0:T(8,128)(2,1)S(1)} %get-tuple-element.35), channel_id=1, source_target_pairs={{0,1},{1,0},{2,5},{3,4},{4,3},{5,2},{6,9},{7,8},{8,7},{9,6},{10,13... | collective-permute-start | bytes 196616 | tf_op jit(solution)/shard_map/ppermute | solution.py:451
  2.0 8.5 %collective-permute-start.1 = (bf16[256,128]{1,0:T(8,128)(2,1)S(1)}, bf16[256,128]{1,0:T(8,128)(2,1)S(1)}, u32[]{:S(2)}, u32[]{:S(2)}) collective-permute-start(bf16[256,128]{1,0:T(8,128)(2,1)S(1)} %get-tuple-element.35), channel_id=1, source_target_pairs={{0,3},{1,2},{2,1},{3,0},{4,7},{5,6},{6,5},{7,4},{8,11},{9,10},{10,... | collective-permute-start | bytes 196616 | tf_op jit(solution)/shard_map/ppermute | solution.py:450
  5.7 4.8 %collective-permute-start = (bf16[256,128]{1,0:T(8,128)(2,1)S(1)}, bf16[256,128]{1,0:T(8,128)(2,1)S(1)}, u32[]{:S(2)}, u32[]{:S(2)}) collective-permute-start(bf16[256,128]{1,0:T(8,128)(2,1)S(1)} %get-tuple-element.36), channel_id=1, source_target_pairs={{0,1},{1,0},{2,3},{3,2},{4,5},{5,4},{6,7},{7,6},{8,9},{9,8},{10,11... | collective-permute-start | bytes 196616 | tf_op jit(solution)/shard_map/ppermute | solution.py:452
  5.7 0.7 %copy-start.1 = (s32[96]{0:T(128)S(1)}, s32[96]{0:T(128)}, u32[]{:S(2)}) copy-start(s32[96]{0:T(128)} %param.6) | copy-start | bytes 1156
  11.1 1.4 %collective-permute-start.3 = (f32[80,128]{1,0:T(8,128)S(1)}, f32[80,128]{1,0:T(8,128)S(1)}, u32[]{:S(2)}, u32[]{:S(2)}) collective-permute-start(f32[80,128]{1,0:T(8,128)S(1)} %get-tuple-element.25), channel_id=1, source_target_pairs={{0,1},{1,0},{2,3},{3,2},{4,5},{5,4},{6,7},{7,6},{8,9},{9,8},{10,11... | collective-permute-start | bytes 122888 | tf_op jit(solution)/shard_map/ppermute | solution.py:273
  12.5 3.4 %collective-permute-start.4 = (f32[80,128]{1,0:T(8,128)S(1)}, f32[80,128]{1,0:T(8,128)S(1)}, u32[]{:S(2)}, u32[]{:S(2)}) collective-permute-start(f32[80,128]{1,0:T(8,128)S(1)} %add.17), channel_id=1, source_target_pairs={{0,3},{1,2},{2,1},{3,0},{4,7},{5,6},{6,5},{7,4},{8,11},{9,10},{10,... | collective-permute-start | bytes 122888 | tf_op jit(solution)/shard_map/ppermute | solution.py:276
  16.0 3.4 %collective-permute-start.5 = (f32[80,128]{1,0:T(8,128)S(1)}, f32[80,128]{1,0:T(8,128)S(1)}, u32[]{:S(2)}, u32[]{:S(2)}) collective-permute-start(f32[80,128]{1,0:T(8,128)S(1)} %add.18), channel_id=1, source_target_pairs={{0,5},{1,4},{2,7},{3,6},{4,1},{5,0},{6,3},{7,2},{8,13},{9,12},{10,... | collective-permute-start | bytes 122888 | tf_op jit(solution)/shard_map/ppermute | solution.py:276
  19.4 4.3 %collective-permute-start.6 = (f32[80,128]{1,0:T(8,128)S(1)}, f32[80,128]{1,0:T(8,128)S(1)}, u32[]{:S(2)}, u32[]{:S(2)}) collective-permute-start(f32[80,128]{1,0:T(8,128)S(1)} %add.19), channel_id=1, source_target_pairs={{0,9},{1,8},{2,11},{3,10},{4,13},{5,12},{6,15},{7,14},{8,1},{9,0},... | collective-permute-start | bytes 122888 | tf_op jit(solution)/shard_map/ppermute | solution.py:276
  23.7 1.2 %collective-permute-start.7 = (f32[80,128]{1,0:T(8,128)S(1)}, f32[80,128]{1,0:T(8,128)S(1)}, u32[]{:S(2)}, u32[]{:S(2)}) collective-permute-start(f32[80,128]{1,0:T(8,128)S(1)} %add.20.kept_ref), channel_id=1, source_target_pairs={{0,1},{1,0},{2,3},{3,2},{4,5},{5,4},{6,7},{7,6},{8,9},{9,8},{10,11... | collective-permute-start | bytes 122888 | tf_op jit(solution)/shard_map/ppermute | solution.py:280
